TPU v7x, 128 devices: a whole 4x4x4 slice. The times are simulated.
128 devices in a mesh: grp: 4 (over y), dev: 32 (over z, x, core).
Axes of the slice: x: 4, y: 4, z: 4, core: 2. Of those that a mesh axis runs over, the one named last changes fastest.
Arguments:
- voltages: bfloat16 [2, 1024, 65536], P(None, 'dev', 'grp'), may hold values from -6 to 6
- history: bfloat16 [2, 1024, 12288], P(None, 'dev'), may hold values from -6 to 6
- pfb_taps: float32 [4, 4096], replicated, may hold values from -3 to 3
- chan_map: int32 [4096], replicated, may hold values from 0 to 4095, each once
- flag_lists: int32 [512, 12], replicated, may hold values from 0 to 4095, as said below
- beam_index: int32 [256, 1024], replicated, may hold values from 0 to 63
- beam_table: float32 [2, 64], replicated, may hold values from -4 to 4
Outputs:
- visibilities: bfloat16 [128, 2, 2, 1024, 1024], P(('grp', 'dev'))
- beam_power: float32 [2, 256, 4096], P(None, None, ('grp', 'dev'))
Inputs may be any that keep to these rules, and one draw needn't show every extreme that they name: `flag_lists`: channel numbers; a list may name a channel twice.
All inputs are finite; a program needn't handle non-finite values.
Results may differ from a plain program's by a relative error of at most 0.0054.
Values may be sent and summed in bfloat16 or wider, within the bound.
A program may use at most 128 MiB of HBM per device.

v0:
```python
import math

import numpy as np

import jax
import jax.numpy as jnp
from jax import lax
from jax.experimental import pallas as pl
from jax.experimental.pallas import tpu as pltpu
from jax.sharding import PartitionSpec as P

N1 = 32
N2 = 128
BLK = N1 * N2
ROWS = 32
VMEM_LIMIT = 48 * 1024 * 1024
NT = (((1,), (1,)), ((), ()))


def tables():
    k1 = np.arange(N1)[:, None]
    n2 = np.arange(N2)[None, :]
    turn = 2.0 * np.pi * ((k1 * n2) % BLK) / BLK
    twist = np.stack([np.cos(turn), np.sin(turn)]).astype(np.float32)
    angle = 2.0 * np.pi * ((np.arange(N2)[:, None] * n2) % N2) / N2
    both = np.concatenate([np.cos(angle), np.sin(angle)], axis=1) / math.sqrt(BLK)
    high = both.astype(jnp.bfloat16)
    low = (both - high.astype(np.float64)).astype(jnp.bfloat16)
    return jnp.asarray(twist), jnp.asarray(np.stack([high, low]))


def add(a, b):
    return (a[0] + b[0], a[1] + b[1])


def sub(a, b):
    return (a[0] - b[0], a[1] - b[1])


def minus_i(a):
    return (a[1], -a[0])


def times(a, c, s):
    return (a[0] * c + a[1] * s, a[1] * c - a[0] * s)


def dft4(x):
    a, b = add(x[0], x[2]), sub(x[0], x[2])
    c, d = add(x[1], x[3]), minus_i(sub(x[1], x[3]))
    return [add(a, c), add(b, d), sub(a, c), sub(b, d)]


def dft8(x):
    even = dft4([x[0], x[2], x[4], x[6]])
    odd = dft4([x[1], x[3], x[5], x[7]])
    h = math.sqrt(0.5)
    o1, o3 = odd[1], odd[3]
    odd = [
        odd[0],
        ((o1[0] + o1[1]) * h, (o1[1] - o1[0]) * h),
        minus_i(odd[2]),
        ((o3[1] - o3[0]) * h, (-o3[0] - o3[1]) * h),
    ]
    return [add(even[k], odd[k]) for k in range(4)] + [sub(even[k], odd[k]) for k in range(4)]


def first_stage(src, lane0, row0, taps_ref, twist_ref, mid, high, low, out_row):
    rows = pl.ds(row0, 16)
    for j in range(4):
        points = []
        for a in range(8):
            n1 = 4 * a + j
            total = [None, None]
            for p in range(4):
                tap = taps_ref[pl.ds(p, 1), pl.ds(n1 * N2, N2)]
                for part in range(2):
                    at = pl.multiple_of(lane0 + p * BLK + n1 * N2, N2)
                    term = tap * src[part, rows, pl.ds(at, N2)].astype(jnp.float32)
                    total[part] = term if p == 0 else total[part] + term
            points.append(tuple(total))
        for k, value in enumerate(dft8(points)):
            if j and k:
                turn = 2.0 * math.pi * j * k / N1
                value = times(value, math.cos(turn), math.sin(turn))
            mid[0, k, j] = value[0]
            mid[1, k, j] = value[1]
    for k in range(8):
        column = dft4([(mid[0, k, j], mid[1, k, j]) for j in range(4)])
        for l, value in enumerate(column):
            k1 = k + 8 * l
            if k1:
                value = times(value, twist_ref[0, pl.ds(k1, 1), :], twist_ref[1, pl.ds(k1, 1), :])
            for dst, (re, im) in zip((high, low), split(value)):
                dst[k1, pl.ds(out_row, 16), pl.ds(0, N2)] = re
                dst[k1, pl.ds(out_row, 16), pl.ds(N2, N2)] = im
                dst[k1, pl.ds(64 + out_row, 16), pl.ds(0, N2)] = im
                dst[k1, pl.ds(64 + out_row, 16), pl.ds(N2, N2)] = -re


def split(value):
    high = tuple(v.astype(jnp.bfloat16) for v in value)
    low = tuple((v - h.astype(jnp.float32)).astype(jnp.bfloat16) for v, h in zip(value, high))
    return high, low


def second_stage(k1, dft_ref, high, low, lines):
    part = lax.dot_general(dft_ref[0], high[k1], NT, preferred_element_type=jnp.float32)
    part += lax.dot_general(dft_ref[1], high[k1], NT, preferred_element_type=jnp.float32)
    part += lax.dot_general(dft_ref[0], low[k1], NT, preferred_element_type=jnp.float32)
    lines[pl.ds(pl.multiple_of(k1 * N2, N2), N2), :] = part


def block_turn(picked):
    turned = picked.T
    lane = lax.broadcasted_iota(jnp.int32, (32, 128), 1)
    low5 = (lane & 32) == 0
    low6 = (lane & 64) == 0
    c = [turned[32 * n : 32 * n + 32] for n in range(4)]

    def swap(x, y, low_lanes, step):
        return (
            jnp.where(low_lanes, x, pltpu.roll(y, step, 1)),
            jnp.where(low_lanes, pltpu.roll(x, 128 - step, 1), y),
        )

    c[0], c[1] = swap(c[0], c[1], low5, 32)
    c[2], c[3] = swap(c[2], c[3], low5, 32)
    c[0], c[2] = swap(c[0], c[2], low6, 64)
    c[1], c[3] = swap(c[1], c[3], low6, 64)
    return c


def spectra_kernel(
    windows, line_ref, own, history, halo, taps_ref, twist_ref, dft_ref, out, src, mid, high, low, lines, picked, sem
):
    grp = lax.axis_index("grp")
    n_grp = lax.axis_size("grp")
    copies = []

    def copy_in(source, start, count, at):
        return pltpu.make_async_copy(
            source.at[:, :, pl.ds(start * BLK, count * BLK)], src.at[:, :, pl.ds(at * BLK, count * BLK)], sem
        )

    def move(*parts):
        for source, start, count, at in parts:
            copy = copy_in(source, start, count, at)
            copy.start()
            copy.wait()

    if windows == (0, 4):
        move((own, 0, 4, 0), (halo, 0, 1, 7))

        @pl.when(grp < n_grp - 1)
        def _():
            move((own, 1, 3, 4))

        @pl.when(grp == n_grp - 1)
        def _():
            move((history, 0, 3, 4))

    else:
        move((own, 0, 3, 2))

        @pl.when(grp > 0)
        def _():
            move((halo, 0, 2, 0))

        @pl.when(grp == 0)
        def _():
            move((history, 1, 2, 0))

    for number, window in enumerate(windows):

        @pl.loop(0, ROWS // 16)
        def _(half):
            row0 = pl.multiple_of(half * 16, 16)
            first_stage(src, window * BLK, row0, taps_ref, twist_ref, mid, high, low, number * 32 + row0)

    @pl.loop(0, N1)
    def _(k1):
        second_stage(k1, dft_ref, high, low, lines)

    @pl.loop(0, 32)
    def _(group):
        for n in range(128):
            picked[pl.ds(n, 1), :] = lines[pl.ds(line_ref[group * 128 + n], 1), :]
        for n, block in enumerate(block_turn(picked[...])):
            out[group * 4 + n] = block.astype(jnp.bfloat16)


def spectra(windows, line, own, history, halo, taps, twist, dft):
    whole = pl.BlockSpec(memory_space=pltpu.VMEM)
    anywhere = pl.BlockSpec(memory_space=pl.ANY)
    return pl.pallas_call(
        lambda *refs: spectra_kernel(windows, *refs),
        out_shape=jax.ShapeDtypeStruct((128, 32, 128), jnp.bfloat16),
        in_specs=[pl.BlockSpec(memory_space=pltpu.SMEM), anywhere, anywhere, anywhere, whole, whole, whole],
        out_specs=whole,
        scratch_shapes=[
            pltpu.VMEM((2, ROWS, 8 * BLK), jnp.bfloat16),
            pltpu.VMEM((2, 8, 4, 16, 128), jnp.float32),
            pltpu.VMEM((N1, 128, 256), jnp.bfloat16),
            pltpu.VMEM((N1, 128, 256), jnp.bfloat16),
            pltpu.VMEM((BLK, 128), jnp.float32),
            pltpu.VMEM((128, 128), jnp.float32),
            pltpu.SemaphoreType.DMA,
        ],
        compiler_params=pltpu.CompilerParams(vmem_limit_bytes=VMEM_LIMIT),
        cost_estimate=pl.CostEstimate(flops=10**10, bytes_accessed=5 * 10**6, transcendentals=0),
        name="spectra",
    )(line, own, history, halo, taps, twist, dft)


def side_kernel(flags_ref, mine_ref, index_ref, table_ref, mask_ref, weight_ref, inverse_ref):
    mine = mine_ref[...]
    flagged = flags_ref[:, 0:1] == mine
    for n in range(1, flags_ref.shape[1]):
        flagged = flagged | (flags_ref[:, n : n + 1] == mine)
    mask = jnp.where(flagged, 0.0, 1.0).astype(jnp.bfloat16)
    mask_ref[...] = mask
    for n in range(4):
        rows = pl.ds(n * 256, 256)
        counts = 2.0 * lax.dot_general(mask_ref[rows, :], mask_ref[...], NT, preferred_element_type=jnp.float32)
        inverse_ref[rows, :] = 1.0 / counts
    scale = 1.0 / math.sqrt(index_ref.shape[1])
    table_re = jnp.broadcast_to(table_ref[0:1, :] * scale, (8, 128))
    table_im = jnp.broadcast_to(table_ref[1:2, :] * scale, (8, 128))

    @pl.loop(0, index_ref.shape[0] // 16)
    def _(step):
        at = pl.multiple_of(step * 16, 16)
        for n in range(index_ref.shape[1] // 128):
            cols = pl.ds(n * 128, 128)
            re, im = [], []
            for half in range(2):
                index = index_ref[pl.ds(at + 8 * half, 8), cols]
                re.append(jnp.take_along_axis(table_re, index, axis=1, mode="promise_in_bounds"))
                im.append(jnp.take_along_axis(table_im, index, axis=1, mode="promise_in_bounds"))
            weight_ref[pl.ds(at, 16), cols] = jnp.concatenate(re, axis=0).astype(jnp.bfloat16)
            weight_ref[pl.ds(256 + at, 16), cols] = jnp.concatenate(im, axis=0).astype(jnp.bfloat16)


def side(flags, mine, index, table):
    whole = pl.BlockSpec(memory_space=pltpu.VMEM)
    return pl.pallas_call(
        side_kernel,
        out_shape=(
            jax.ShapeDtypeStruct((1024, 128), jnp.bfloat16),
            jax.ShapeDtypeStruct((512, 1024), jnp.bfloat16),
            jax.ShapeDtypeStruct((1024, 1024), jnp.float32),
        ),
        in_specs=[whole] * 4,
        out_specs=(whole,) * 3,
        compiler_params=pltpu.CompilerParams(vmem_limit_bytes=VMEM_LIMIT),
        cost_estimate=pl.CostEstimate(flops=3 * 10**9, bytes_accessed=6 * 10**6, transcendentals=0),
        name="side",
    )(flags, mine, index, table)


def correlate_kernel(later, earlier, mask_ref, weight_ref, inverse_ref, vis_ref, power_ref, left, right):
    step = pl.program_id(0)
    lane = lax.broadcasted_iota(jnp.int32, (256, 128), 1)
    real_lane = lane < 64

    @pl.when(step == 0)
    def _():
        @pl.loop(0, 4)
        def _(n):
            rows = pl.ds(pl.multiple_of(n * 256, 256), 256)
            mask = mask_ref[rows, :].astype(jnp.float32)
            first = (lane & 32) == 0
            one = later[1, rows, :].astype(jnp.float32)
            three = later[3, rows, :].astype(jnp.float32)
            blocks = (
                (later[0, rows, :], earlier[0, rows, :], earlier[1, rows, :], jnp.where(first, one, three)),
                (later[2, rows, :], earlier[2, rows, :], earlier[3, rows, :], jnp.where(first, three, one)),
            )
            for t in range(2):
                for b in range(4):
                    masked = blocks[t][b].astype(jnp.float32) * mask
                    crossed = pltpu.roll(masked, 64, 1)
                    left[t, rows, pl.ds(b * 128, 128)] = masked.astype(jnp.bfloat16)
                    right[t, rows, pl.ds(b * 128, 128)] = jnp.where(real_lane, crossed, -crossed).astype(jnp.bfloat16)

        for t in range(2):
            total = jnp.zeros((256, 128), jnp.float32)
            product = jnp.dot(weight_ref[...], left[t], preferred_element_type=jnp.float32)
            for b in range(4):
                by_real = product[:256, b * 128 : b * 128 + 128]
                by_imag = pltpu.roll(product[256:, b * 128 : b * 128 + 128], 64, 1)
                beam = by_real + jnp.where(real_lane, -by_imag, by_imag)
                total += beam * beam
            total += pltpu.roll(total, 64, 1)
            total += pltpu.roll(total, 32, 1)
            power_ref[t] = total[:, :32] * 0.125

    rows = pl.ds(pl.multiple_of(step * 256, 256), 256)
    inverse = inverse_ref[...]
    for t in range(2):
        for part, lhs in enumerate((left, right)):
            value = lax.dot_general(lhs[t, rows, :], left[t], NT, preferred_element_type=jnp.float32)
            vis_ref[0, t, part] = (value * inverse).astype(jnp.bfloat16)


def correlate(later, earlier, mask, weight, inverse):
    return pl.pallas_call(
        correlate_kernel,
        grid=(4,),
        out_shape=(
            jax.ShapeDtypeStruct((1, 2, 2, 1024, 1024), jnp.bfloat16),
            jax.ShapeDtypeStruct((2, 256, 32), jnp.float32),
        ),
        in_specs=[
            pl.BlockSpec((4, 1024, 128), lambda i: (0, 0, 0)),
            pl.BlockSpec((4, 1024, 128), lambda i: (0, 0, 0)),
            pl.BlockSpec((1024, 128), lambda i: (0, 0)),
            pl.BlockSpec((512, 1024), lambda i: (0, 0)),
            pl.BlockSpec((256, 1024), lambda i: (i, 0)),
        ],
        out_specs=(
            pl.BlockSpec((1, 2, 2, 256, 1024), lambda i: (0, 0, 0, i, 0)),
            pl.BlockSpec((2, 256, 32), lambda i: (0, 0, 0)),
        ),
        scratch_shapes=[pltpu.VMEM((2, 1024, 512), jnp.bfloat16)] * 2,
        compiler_params=pltpu.CompilerParams(vmem_limit_bytes=VMEM_LIMIT),
        cost_estimate=pl.CostEstimate(flops=6 * 10**9, bytes_accessed=16 * 10**6, transcendentals=0),
        name="correlate",
    )(later, earlier, mask, weight, inverse)


def per_device(voltages, history, pfb_taps, chan_map, flag_lists, beam_index, beam_table):
    n_grp = lax.axis_size("grp")
    n_dev = lax.axis_size("dev")
    twist, dft = tables()
    after = lax.ppermute(voltages[:, :, :BLK], "grp", [(n, (n - 1) % n_grp) for n in range(n_grp)])
    before = lax.ppermute(voltages[:, :, 2 * BLK :], "grp", [(n, n + 1) for n in range(n_grp - 1)])
    line = (chan_map % N1) * N2 + chan_map // N1
    later = spectra((0, 4), line, voltages, history, after, pfb_taps, twist, dft)
    later = lax.all_to_all(later, ("grp", "dev"), split_axis=0, concat_axis=0, tiled=True)
    earlier = spectra((0, 1), line, voltages, history, before, pfb_taps, twist, dft)
    earlier = lax.all_to_all(earlier, ("grp", "dev"), split_axis=0, concat_axis=0, tiled=True)

    my_bin = lax.axis_index("grp") * n_dev + lax.axis_index("dev")
    mine = jnp.tile(lax.dynamic_slice_in_dim(chan_map, my_bin * 32, 32), 4)[None, :]
    table = jnp.pad(beam_table, ((0, 0), (0, 64)))
    mask, weight, inverse = side(jnp.repeat(flag_lists, 2, axis=0), mine, beam_index, table)
    return correlate(later.reshape(4, 1024, 128), earlier.reshape(4, 1024, 128), mask, weight, inverse)


def solution(mesh):
    placed = (P(None, "dev", "grp"), P(None, "dev", None), P(), P(), P(), P(), P())
    return jax.shard_map(
        per_device,
        mesh=mesh,
        in_specs=placed,
        out_specs=(P(("grp", "dev"), None, None, None, None), P(None, None, ("grp", "dev"))),
        check_vma=False,
    )
```

profile of v0, /device:TPU:1, one launch (start us, length us, event | category | flops | bytes accessed | tf_op | source)
XLA Modules:
  0.0 122.3 jit_solution(8280858284239516536)
XLA Ops:
  0.6 1.1 slice.6
  1.7 3.6 %collective-permute-start = (bf16[2,32,4096]{2,1,0:T(8,128)(2,1)S(1)}, bf16[2,32,4096]{2,1,0:T(8,128)(2,1)S(1)}, u32[]{:S(2)}, u32[]{:S(2)}) collective-permute-start(bf16[2,32,4096]{2,1,0:T(8,128)(2,1)S(1)} %slice.6), channel_id=1, source_target_pairs={{0,96},{32,0},{64,32},{96,64},{1,97},{33,1},{65,33},{97,65},{2,98}... | collective-permute-start | bytes 1572872 | tf_op jit(solution)/shard_map/ppermute | solution.py:337
  5.3 2.3 %slice.7 = bf16[2,32,8192]{2,1,0:T(8,128)(2,1)} slice(bf16[2,32,16384]{2,1,0:T(8,128)(2,1)} %refs_1_.3), slice={[0:2], [0:32], [8192:16384]} | slice | bytes 2097152 | tf_op jit(solution)/shard_map/slice | solution.py:338
  7.6 2.3 %collective-permute-start.1 = (bf16[2,32,8192]{2,1,0:T(8,128)(2,1)}, bf16[2,32,8192]{2,1,0:T(8,128)(2,1)}, u32[]{:S(2)}, u32[]{:S(2)}) collective-permute-start(bf16[2,32,8192]{2,1,0:T(8,128)(2,1)} %slice.7), channel_id=1, source_target_pairs={{0,32},{32,64},{64,96},{1,33},{33,65},{65,97},{2,34},{34,66},{66,9... | collective-permute-start | bytes 3145736 | tf_op jit(solution)/shard_map/ppermute | solution.py:338
  9.9 0.7 fusion.1.refs_0_
  10.6 5.3 %collective-permute-done.refs_3_ = bf16[2,32,4096]{2,1,0:T(8,128)(2,1)S(1)} collective-permute-done((bf16[2,32,4096]{2,1,0:T(8,128)(2,1)S(1)}, bf16[2,32,4096]{2,1,0:T(8,128)(2,1)S(1)}, u32[]{:S(2)}, u32[]{:S(2)}) %collective-permute-start) | collective-permute-done | bytes 524320 | tf_op jit(solution)/shard_map/ppermute | solution.py:337
  15.9 1.6 %copy-done = bf16[2,32,16384]{2,1,0:T(8,128)(2,1)S(1)} copy-done((bf16[2,32,16384]{2,1,0:T(8,128)(2,1)S(1)}, bf16[2,32,16384]{2,1,0:T(8,128)(2,1)}, u32[]{:S(2)}) %copy-start) | copy-done | bytes 2097176
  17.5 1.4 %copy-done.4 = bf16[2,32,12288]{2,1,0:T(8,128)(2,1)S(1)} copy-done((bf16[2,32,12288]{2,1,0:T(8,128)(2,1)S(1)}, bf16[2,32,12288]{2,1,0:T(8,128)(2,1)}, u32[]{:S(2)}) %copy-start.4) | copy-done | bytes 1572888
  18.9 0.8 copy-done.7
  19.8 0.9 copy-done.9
  20.7 0.8 copy-done.11
  21.4 21.0 %spectra.2 = bf16[128,32,128]{2,1,0:T(8,128)(2,1)S(1)} custom-call(s32[4096]{0:T(1024)S(1)} %fusion.1.refs_0_, bf16[2,32,16384]{2,1,0:T(8,128)(2,1)S(1)} %copy-done, bf16[2,32,12288]{2,1,0:T(8,128)(2,1)S(1)} %copy-done.4, bf16[2,32,4096]{2,1,0:T(8,128)(2,1)S(1)} %collective-permute-done.refs_3_, f32[4,4096]{1,0:T(4,128)S(1)} %copy-done.7, ...), custom_call_target="tpu_custom_call" | custom-call | flops 10000000000 | bytes 5000000 | tf_op jit(solution)/shard_map/spectra/pallas_call | solution.py:196
  42.5 0.0 copy-start.3
  42.5 1.0 copy-done.3
  43.4 12.0 %all-to-all-start = ((bf16[128,32,128]{2,1,0:T(8,128)(2,1)}), bf16[128,32,128]{2,1,0:T(8,128)(2,1)S(1)}, u32[]{:S(2)}, u32[]{:S(2)}) async-start(bf16[128,32,128]{2,1,0:T(8,128)(2,1)} %copy-done.3), calls=%async_computation | async-start | bytes 2097152 | tf_op jit(solution)/shard_map/all_to_all | solution.py:341
  55.5 0.0 copy-start.5
  55.6 1.4 %copy-done.5 = bf16[2,32,12288]{2,1,0:T(8,128)(2,1)S(1)} copy-done((bf16[2,32,12288]{2,1,0:T(8,128)(2,1)S(1)}, bf16[2,32,12288]{2,1,0:T(8,128)(2,1)}, u32[]{:S(2)}) %copy-start.5) | copy-done | bytes 1572888
  57.0 20.9 %spectra.3 = bf16[128,32,128]{2,1,0:T(8,128)(2,1)S(1)} custom-call(s32[4096]{0:T(1024)S(1)} %fusion.1.refs_0_, bf16[2,32,16384]{2,1,0:T(8,128)(2,1)S(1)} %copy-done.1, bf16[2,32,12288]{2,1,0:T(8,128)(2,1)S(1)} %copy-done.5, bf16[2,32,8192]{2,1,0:T(8,128)(2,1)} %collective-permute-done.1.refs_3_, f32[4,4096]{1,0:T(4,128)S(1)} %copy-done.8, ...), custom_call_target="tpu_custom_call" | custom-call | flops 10000000000 | bytes 5000000 | tf_op jit(solution)/shard_map/spectra/pallas_call | solution.py:196
  77.9 1.0 copy-done.2
  78.9 10.9 %all-to-all-start.1 = ((bf16[128,32,128]{2,1,0:T(8,128)(2,1)}), bf16[128,32,128]{2,1,0:T(8,128)(2,1)S(1)}, u32[]{:S(2)}, u32[]{:S(2)}) async-start(bf16[128,32,128]{2,1,0:T(8,128)(2,1)} %copy-done.2), calls=%async_computation.1 | async-start | bytes 2097152 | tf_op jit(solution)/shard_map/all_to_all | solution.py:343
  89.8 0.8 dynamic_slice.3
  90.6 0.1 broadcast_in_dim_tile.3.mine_ref
  90.7 0.1 copy.11
  90.8 0.2 broadcast_in_dim.3
  91.0 0.0 copy-start.6
  91.0 1.2 copy-done.6
  92.3 6.5 %side.1 = (bf16[1024,128]{1,0:T(8,128)(2,1)S(1)}, bf16[512,1024]{1,0:T(8,128)(2,1)S(1)}, f32[1024,1024]{1,0:T(8,128)}) custom-call(s32[1024,12]{1,0:T(8,128)S(1)} %bitcast.5, s32[1,128]{1,0:T(1,128)S(1)} %broadcast_in_dim_tile.3.mine_ref, s32[256,1024]{1,0:T(8,128)S(1)} %copy-done.6, f32[2,128]{1,0:T(2,128)S(1)} %pad.4.table_ref), custom_call_target="tpu_custom_call" | custom-call | flops 3000000000 | bytes 6000000 | tf_op jit(solution)/shard_map/side/pallas_call | solution.py:247
  98.7 0.7 copy-done.13
  99.4 9.7 %all-to-all-done.1 = bf16[128,32,128]{2,1,0:T(8,128)(2,1)S(1)} async-done(((bf16[128,32,128]{2,1,0:T(8,128)(2,1)}), bf16[128,32,128]{2,1,0:T(8,128)(2,1)S(1)}, u32[]{:S(2)}, u32[]{:S(2)}) %all-to-all-start.1) | async-done | bytes 1048608 | tf_op jit(solution)/shard_map/all_to_all | solution.py:343
  109.1 0.9 copy-done.14
  110.1 11.4 %correlate.1 = (bf16[1,2,2,1024,1024]{4,3,2,1,0:T(8,128)(2,1)}, f32[2,256,32]{2,1,0:T(8,128)S(1)}) custom-call(bf16[4,1024,128]{2,1,0:T(8,128)(2,1)S(1)} %bitcast.3, bf16[4,1024,128]{2,1,0:T(8,128)(2,1)S(1)} %bitcast.4, bf16[1024,128]{1,0:T(8,128)(2,1)S(1)} %copy-done.14, bf16[512,1024]{1,0:T(8,128)(2,1)S(1)} %get-tuple-element.6.weight_ref, ...), custom_call_target="tpu_custom_call" | custom-call | flops 6000000000 | bytes 16000000 | tf_op jit(solution)/shard_map/correlate/pallas_call | solution.py:308
  121.5 0.7 copy.12
  (24 shorter events, 0.1 us)
Async XLA Ops:
  1.7 14.2 %collective-permute-start = (bf16[2,32,4096]{2,1,0:T(8,128)(2,1)S(1)}, bf16[2,32,4096]{2,1,0:T(8,128)(2,1)S(1)}, u32[]{:S(2)}, u32[]{:S(2)}) collective-permute-start(bf16[2,32,4096]{2,1,0:T(8,128)(2,1)S(1)} %slice.6), channel_id=1, source_target_pairs={{0,96},{32,0},{64,32},{96,64},{1,97},{33,1},{65,33},{97,65},{2,98}... | collective-permute-start | bytes 1572872 | tf_op jit(solution)/shard_map/ppermute | solution.py:337
  7.6 47.9 %collective-permute-start.1 = (bf16[2,32,8192]{2,1,0:T(8,128)(2,1)}, bf16[2,32,8192]{2,1,0:T(8,128)(2,1)}, u32[]{:S(2)}, u32[]{:S(2)}) collective-permute-start(bf16[2,32,8192]{2,1,0:T(8,128)(2,1)} %slice.7), channel_id=1, source_target_pairs={{0,32},{32,64},{64,96},{1,33},{33,65},{65,97},{2,34},{34,66},{66,9... | collective-permute-start | bytes 3145736 | tf_op jit(solution)/shard_map/ppermute | solution.py:338
  15.9 1.6 %copy-start = (bf16[2,32,16384]{2,1,0:T(8,128)(2,1)S(1)}, bf16[2,32,16384]{2,1,0:T(8,128)(2,1)}, u32[]{:S(2)}) copy-start(bf16[2,32,16384]{2,1,0:T(8,128)(2,1)} %refs_1_.3) | copy-start | bytes 6291460
  17.5 1.4 %copy-start.4 = (bf16[2,32,12288]{2,1,0:T(8,128)(2,1)S(1)}, bf16[2,32,12288]{2,1,0:T(8,128)(2,1)}, u32[]{:S(2)}) copy-start(bf16[2,32,12288]{2,1,0:T(8,128)(2,1)} %refs_2_.3) | copy-start | bytes 4718596
  18.9 0.8 copy-start.7
  19.8 0.9 copy-start.9
  20.7 0.8 copy-start.11
  21.4 34.1 %copy-start.1 = (bf16[2,32,16384]{2,1,0:T(8,128)(2,1)S(1)}, bf16[2,32,16384]{2,1,0:T(8,128)(2,1)}, u32[]{:S(2)}) copy-start(bf16[2,32,16384]{2,1,0:T(8,128)(2,1)} %refs_1_.3) | copy-start | bytes 6291460
  21.4 34.1 %copy-start.8 = (f32[4,4096]{1,0:T(4,128)S(1)}, f32[4,4096]{1,0:T(4,128)}, u32[]{:S(2)}) copy-start(f32[4,4096]{1,0:T(4,128)} %refs_4_.3) | copy-start | bytes 196612
  21.4 34.1 %copy-start.10 = (bf16[2,128,256]{2,1,0:T(8,128)(2,1)S(1)}, bf16[2,128,256]{2,1,0:T(8,128)(2,1)}, u32[]{:S(2)}) copy-start(bf16[2,128,256]{2,1,0:T(8,128)(2,1)} %constant.49.clone.refs_6_) | copy-start | bytes 393220
  21.4 34.1 %copy-start.12 = (f32[2,32,128]{2,1,0:T(8,128)S(1)}, f32[2,32,128]{2,1,0:T(8,128)}, u32[]{:S(2)}) copy-start(f32[2,32,128]{2,1,0:T(8,128)} %constant.48.clone.refs_5_) | copy-start | bytes 98308
  42.5 1.0 copy-start.3
  43.4 35.4 %all-to-all-start = ((bf16[128,32,128]{2,1,0:T(8,128)(2,1)}), bf16[128,32,128]{2,1,0:T(8,128)(2,1)S(1)}, u32[]{:S(2)}, u32[]{:S(2)}) async-start(bf16[128,32,128]{2,1,0:T(8,128)(2,1)} %copy-done.3), calls=%async_computation | async-start | bytes 2097152 | tf_op jit(solution)/shard_map/all_to_all | solution.py:341
  55.5 1.4 %copy-start.5 = (bf16[2,32,12288]{2,1,0:T(8,128)(2,1)S(1)}, bf16[2,32,12288]{2,1,0:T(8,128)(2,1)}, u32[]{:S(2)}) copy-start(bf16[2,32,12288]{2,1,0:T(8,128)(2,1)} %refs_2_.3) | copy-start | bytes 4718596
  57.0 33.7 %copy-start.15 = (s32[512,12]{0,1:T(8,128)S(1)}, s32[512,12]{0,1:T(8,128)}, u32[]{:S(2)}) copy-start(s32[512,12]{0,1:T(8,128)} %param.13) | copy-start | bytes 73732
  57.0 33.9 %copy-start.16 = (f32[2,64]{1,0:T(2,128)S(1)}, f32[2,64]{1,0:T(2,128)}, u32[]{:S(2)}) copy-start(f32[2,64]{1,0:T(2,128)} %param.15) | copy-start | bytes 1540
  77.9 1.0 copy-start.2
  78.9 30.3 %all-to-all-start.1 = ((bf16[128,32,128]{2,1,0:T(8,128)(2,1)}), bf16[128,32,128]{2,1,0:T(8,128)(2,1)S(1)}, u32[]{:S(2)}, u32[]{:S(2)}) async-start(bf16[128,32,128]{2,1,0:T(8,128)(2,1)} %copy-done.2), calls=%async_computation.1 | async-start | bytes 2097152 | tf_op jit(solution)/shard_map/all_to_all | solution.py:343
  91.0 1.2 %copy-start.6 = (s32[256,1024]{1,0:T(8,128)S(1)}, s32[256,1024]{1,0:T(8,128)}, u32[]{:S(2)}) copy-start(s32[256,1024]{1,0:T(8,128)} %index_ref.1) | copy-start | bytes 3145732
  98.7 0.7 copy-start.13
  109.1 1.0 copy-start.14
where the time goes:
time: 123 us; the launch traced here: 122 us
  Pallas kernels  59.8 us (49%)
  starting transfers between devices  28.8 us (23%)
  local copies, waits for them, and re-layouts  17 us (14%)
  waiting for transfers between devices  15 us (12%)
    pallas_call x2, Pallas kernels, spectra(): pl.pallas_call(lambda *refs: spectra_kernel(windows, *refs), out_shape=ja...  41.9 us
    all_to_all x1, starting transfers between devices, per_device(): lax.all_to_all(later, ('grp', 'dev'), split_axis=0, concat_axis=0, tiled=...  12 us
    unnamed x35, local copies, waits for them, and re-layouts  11.9 us
    pallas_call x1, Pallas kernels, correlate(): pl.pallas_call(correlate_kernel, grid=(4,), out_shape=(jax.ShapeDtypeStru...  11.4 us
    all_to_all x1, starting transfers between devices, per_device(): lax.all_to_all(earlier, ('grp', 'dev'), split_axis=0, concat_axis=0, tile...  10.9 us
    all_to_all x1, waiting for transfers between devices, per_device(): lax.all_to_all(earlier, ('grp', 'dev'), split_axis=0, concat_axis=0, tile...  9.72 us
    pallas_call x1, Pallas kernels, side(): pl.pallas_call(side_kernel, out_shape=(jax.ShapeDtypeStruct((1024, 128),...  6.47 us
    ppermute x1, waiting for transfers between devices, per_device(): lax.ppermute(voltages[:, :, :BLK], 'grp', [(n, (n - 1) % n_grp) for n in...  5.31 us
  transfers between devices with their start and end apart: 4, of which 2 were waited for; matrix products, arithmetic and copies ran while one was open for 3% of the time, Pallas kernels for 40%

commit v1 on v0

--- a/solution.py
+++ b/solution.py
@@ -13,6 +13,7 @@
 N2 = 128
 BLK = N1 * N2
 ROWS = 32
+FIRST_LIMIT = 60 * 1024 * 1024
 VMEM_LIMIT = 48 * 1024 * 1024
 NT = (((1,), (1,)), ((), ()))
 
@@ -108,11 +109,11 @@
     part = lax.dot_general(dft_ref[0], high[k1], NT, preferred_element_type=jnp.float32)
     part += lax.dot_general(dft_ref[1], high[k1], NT, preferred_element_type=jnp.float32)
     part += lax.dot_general(dft_ref[0], low[k1], NT, preferred_element_type=jnp.float32)
-    lines[pl.ds(pl.multiple_of(k1 * N2, N2), N2), :] = part
+    lines[pl.ds(k1, N2, stride=N1), :] = part
 
 
 def block_turn(picked):
-    turned = picked.T
+    turned = picked.astype(jnp.bfloat16).T
     lane = lax.broadcasted_iota(jnp.int32, (32, 128), 1)
     low5 = (lane & 32) == 0
     low6 = (lane & 64) == 0
@@ -131,102 +132,30 @@
     return c
 
 
-def spectra_kernel(
-    windows, line_ref, own, history, halo, taps_ref, twist_ref, dft_ref, out, src, mid, high, low, lines, picked, sem
-):
-    grp = lax.axis_index("grp")
-    n_grp = lax.axis_size("grp")
-    copies = []
-
-    def copy_in(source, start, count, at):
-        return pltpu.make_async_copy(
-            source.at[:, :, pl.ds(start * BLK, count * BLK)], src.at[:, :, pl.ds(at * BLK, count * BLK)], sem
-        )
-
-    def move(*parts):
-        for source, start, count, at in parts:
-            copy = copy_in(source, start, count, at)
-            copy.start()
-            copy.wait()
-
-    if windows == (0, 4):
-        move((own, 0, 4, 0), (halo, 0, 1, 7))
-
-        @pl.when(grp < n_grp - 1)
-        def _():
-            move((own, 1, 3, 4))
-
-        @pl.when(grp == n_grp - 1)
-        def _():
-            move((history, 0, 3, 4))
-
-    else:
-        move((own, 0, 3, 2))
-
-        @pl.when(grp > 0)
-        def _():
-            move((halo, 0, 2, 0))
-
-        @pl.when(grp == 0)
-        def _():
-            move((history, 1, 2, 0))
-
-    for number, window in enumerate(windows):
-
-        @pl.loop(0, ROWS // 16)
-        def _(half):
-            row0 = pl.multiple_of(half * 16, 16)
-            first_stage(src, window * BLK, row0, taps_ref, twist_ref, mid, high, low, number * 32 + row0)
-
-    @pl.loop(0, N1)
-    def _(k1):
-        second_stage(k1, dft_ref, high, low, lines)
-
-    @pl.loop(0, 32)
-    def _(group):
-        for n in range(128):
-            picked[pl.ds(n, 1), :] = lines[pl.ds(line_ref[group * 128 + n], 1), :]
-        for n, block in enumerate(block_turn(picked[...])):
-            out[group * 4 + n] = block.astype(jnp.bfloat16)
-
-
-def spectra(windows, line, own, history, halo, taps, twist, dft):
-    whole = pl.BlockSpec(memory_space=pltpu.VMEM)
-    anywhere = pl.BlockSpec(memory_space=pl.ANY)
-    return pl.pallas_call(
-        lambda *refs: spectra_kernel(windows, *refs),
-        out_shape=jax.ShapeDtypeStruct((128, 32, 128), jnp.bfloat16),
-        in_specs=[pl.BlockSpec(memory_space=pltpu.SMEM), anywhere, anywhere, anywhere, whole, whole, whole],
-        out_specs=whole,
-        scratch_shapes=[
-            pltpu.VMEM((2, ROWS, 8 * BLK), jnp.bfloat16),
-            pltpu.VMEM((2, 8, 4, 16, 128), jnp.float32),
-            pltpu.VMEM((N1, 128, 256), jnp.bfloat16),
-            pltpu.VMEM((N1, 128, 256), jnp.bfloat16),
-            pltpu.VMEM((BLK, 128), jnp.float32),
-            pltpu.VMEM((128, 128), jnp.float32),
-            pltpu.SemaphoreType.DMA,
-        ],
-        compiler_params=pltpu.CompilerParams(vmem_limit_bytes=VMEM_LIMIT),
-        cost_estimate=pl.CostEstimate(flops=10**10, bytes_accessed=5 * 10**6, transcendentals=0),
-        name="spectra",
-    )(line, own, history, halo, taps, twist, dft)
-
-
-def side_kernel(flags_ref, mine_ref, index_ref, table_ref, mask_ref, weight_ref, inverse_ref):
-    mine = mine_ref[...]
+def side_work(my_bin, chan_ref, flags_ref, index_ref, table_ref, mask_ref, weight_ref, inverse_ref, twice):
+    lane = lax.broadcasted_iota(jnp.int32, (8, 128), 1) & 31
+    mine = jnp.zeros((8, 128), jnp.int32)
+    for q in range(32):
+        mine = jnp.where(lane == q, chan_ref[my_bin * 32 + q], mine)
+    mine = mine[0:1]
     flagged = flags_ref[:, 0:1] == mine
     for n in range(1, flags_ref.shape[1]):
         flagged = flagged | (flags_ref[:, n : n + 1] == mine)
-    mask = jnp.where(flagged, 0.0, 1.0).astype(jnp.bfloat16)
-    mask_ref[...] = mask
-    for n in range(4):
-        rows = pl.ds(n * 256, 256)
+    clean = jnp.where(flagged, 0.0, 1.0)
+    twice[pl.ds(0, 512, stride=2), :] = clean
+    twice[pl.ds(1, 512, stride=2), :] = clean
+    mask_ref[...] = twice[...].astype(jnp.bfloat16)
+
+    @pl.loop(0, 8)
+    def _(n):
+        rows = pl.ds(pl.multiple_of(n * 128, 128), 128)
         counts = 2.0 * lax.dot_general(mask_ref[rows, :], mask_ref[...], NT, preferred_element_type=jnp.float32)
         inverse_ref[rows, :] = 1.0 / counts
+
     scale = 1.0 / math.sqrt(index_ref.shape[1])
-    table_re = jnp.broadcast_to(table_ref[0:1, :] * scale, (8, 128))
-    table_im = jnp.broadcast_to(table_ref[1:2, :] * scale, (8, 128))
+    table = jnp.concatenate([table_ref[...], table_ref[...]], axis=1) * scale
+    table_re = jnp.broadcast_to(table[0:1, :], (8, 128))
+    table_im = jnp.broadcast_to(table[1:2, :], (8, 128))
 
     @pl.loop(0, index_ref.shape[0] // 16)
     def _(step):
@@ -242,24 +171,203 @@
             weight_ref[pl.ds(256 + at, 16), cols] = jnp.concatenate(im, axis=0).astype(jnp.bfloat16)
 
 
-def side(flags, mine, index, table):
+def spectra_kernel(
+    chan_ref, own, history, taps_hbm, twist_hbm, dft_hbm, flags_hbm, index_hbm, table_ref,
+    arrived, mask_ref, weight_ref, inverse_ref,
+    src, mid, high, low, lines, picked, out, taps_ref, twist_ref, dft_ref, flags_ref, index_ref, twice,
+    load_sem, own_sem, rim_sem, halo_send, halo_recv, send_sem, recv_sem,
+):
+    grp, dev = lax.axis_index("grp"), lax.axis_index("dev")
+    n_grp, n_dev = lax.axis_size("grp"), lax.axis_size("dev")
+    count = n_grp * n_dev
+    me = grp * n_dev + dev
+    left, right = lax.rem(grp + n_grp - 1, n_grp), lax.rem(grp + 1, n_grp)
+    is_first, is_last = grp == 0, grp == n_grp - 1
+    barrier = pltpu.get_barrier_semaphore()
+
+    @pl.loop(1, count)
+    def _(n):
+        peer = lax.rem(me + n, count)
+        pl.semaphore_signal(
+            barrier, inc=1, device_id=(peer // n_dev, lax.rem(peer, n_dev)), device_id_type=pl.DeviceIdType.MESH
+        )
+
+    def blocks(ref, start, number):
+        return ref.at[:, :, pl.ds(pl.multiple_of(start * BLK, BLK), number * BLK)]
+
+    loads = [
+        pltpu.make_async_copy(taps_hbm, taps_ref, load_sem.at[0]),
+        pltpu.make_async_copy(twist_hbm, twist_ref, load_sem.at[1]),
+        pltpu.make_async_copy(dft_hbm, dft_ref, load_sem.at[2]),
+        pltpu.make_async_copy(flags_hbm, flags_ref, load_sem.at[3]),
+        pltpu.make_async_copy(index_hbm, index_ref, load_sem.at[4]),
+        pltpu.make_async_copy(own, blocks(src, 2, 4), own_sem),
+    ]
+    for load in reversed(loads):
+        load.start()
+    rim_first = pltpu.make_async_copy(blocks(history, 1, 2), blocks(src, 0, 2), rim_sem)
+    rim_last = pltpu.make_async_copy(blocks(history, 0, 3), blocks(src, 7, 3), rim_sem)
+
+    @pl.when(is_first)
+    def _():
+        rim_first.start()
+
+    @pl.when(is_last)
+    def _():
+        rim_last.start()
+
+    def halo(block, at, slot, target):
+        return pltpu.make_async_remote_copy(
+            src_ref=blocks(own, block, 1),
+            dst_ref=blocks(src, at, 1),
+            send_sem=halo_send.at[slot],
+            recv_sem=halo_recv.at[slot],
+            device_id=(target, dev),
+            device_id_type=pl.DeviceIdType.MESH,
+        )
+
+    after = halo(0, jnp.where(is_first, 10, 6), 0, left)
+    near = halo(3, 1, 1, right)
+    far = halo(2, 0, 2, right)
+
+    pl.semaphore_wait(barrier, count - 1)
+    after.start()
+
+    @pl.when(jnp.logical_not(is_last))
+    def _():
+        near.start()
+        far.start()
+
+    for load in loads:
+        load.wait()
+
+    def filtered(window, line):
+        @pl.loop(0, ROWS // 16)
+        def _(half):
+            row0 = pl.multiple_of(half * 16, 16)
+            first_stage(src, window * BLK, row0, taps_ref, twist_ref, mid, high, low, line + row0)
+
+    def finish(batch):
+        @pl.loop(0, N1 // 4)
+        def _(step):
+            for n in range(4):
+                second_stage(step * 4 + n, dft_ref, high, low, lines)
+
+        @pl.loop(0, 8)
+        def _(step):
+            at = lax.rem(step + me // 16, 8) * 16
+            for part in range(4):
+                for n in range(128):
+                    row = chan_ref[(at + part * 4) * 32 + n]
+                    picked[part, pl.ds(n, 1), :] = lines[pl.ds(row, 1), :]
+                for n, block in enumerate(block_turn(picked[part])):
+                    out[batch, at + part * 4 + n] = block.astype(jnp.bfloat16)
+
+            @pl.loop(0, 16)
+            def _(n):
+                peer = at + n
+
+                @pl.when(peer != me)
+                def _():
+                    pltpu.make_async_remote_copy(
+                        src_ref=out.at[batch, peer],
+                        dst_ref=arrived.at[batch, me],
+                        send_sem=send_sem.at[batch],
+                        recv_sem=recv_sem.at[batch],
+                        device_id=(peer // n_dev, lax.rem(peer, n_dev)),
+                        device_id_type=pl.DeviceIdType.MESH,
+                    ).start()
+
+                @pl.when(peer == me)
+                def _():
+                    pltpu.make_async_copy(out.at[batch, me], arrived.at[batch, me], recv_sem.at[batch]).start()
+
+    filtered(2, 0)
+    side_work(me, chan_ref, flags_ref, index_ref, table_ref, mask_ref, weight_ref, inverse_ref, twice)
+
+    @pl.when(is_last)
+    def _():
+        rim_last.wait()
+
+    after.wait_recv()
+    filtered(jnp.where(is_last, 7, 3), 32)
+    finish(0)
+
+    @pl.when(is_first)
+    def _():
+        rim_first.wait()
+
+    @pl.when(jnp.logical_not(is_first))
+    def _():
+        near.wait_recv()
+
+    filtered(1, 32)
+
+    @pl.when(jnp.logical_not(is_first))
+    def _():
+        far.wait_recv()
+
+    filtered(0, 0)
+    finish(1)
+
+    after.wait_send()
+
+    @pl.when(jnp.logical_not(is_last))
+    def _():
+        near.wait_send()
+        far.wait_send()
+
+    for batch in range(2):
+        sent = out.at[batch, pl.ds(0, count - 1)]
+        pltpu.make_async_copy(sent, sent, send_sem.at[batch]).wait()
+        pltpu.make_async_copy(arrived.at[batch], arrived.at[batch], recv_sem.at[batch]).wait()
+
+
+def spectra(chan_map, voltages, history, taps, twist, dft, flags, index, table):
     whole = pl.BlockSpec(memory_space=pltpu.VMEM)
+    anywhere = pl.BlockSpec(memory_space=pl.ANY)
     return pl.pallas_call(
-        side_kernel,
+        spectra_kernel,
         out_shape=(
+            jax.ShapeDtypeStruct((2, 128, 32, 128), jnp.bfloat16),
             jax.ShapeDtypeStruct((1024, 128), jnp.bfloat16),
             jax.ShapeDtypeStruct((512, 1024), jnp.bfloat16),
             jax.ShapeDtypeStruct((1024, 1024), jnp.float32),
         ),
-        in_specs=[whole] * 4,
-        out_specs=(whole,) * 3,
-        compiler_params=pltpu.CompilerParams(vmem_limit_bytes=VMEM_LIMIT),
-        cost_estimate=pl.CostEstimate(flops=3 * 10**9, bytes_accessed=6 * 10**6, transcendentals=0),
-        name="side",
-    )(flags, mine, index, table)
-
-
-def correlate_kernel(later, earlier, mask_ref, weight_ref, inverse_ref, vis_ref, power_ref, left, right):
+        in_specs=[pl.BlockSpec(memory_space=pltpu.SMEM)] + [anywhere] * 7 + [whole],
+        out_specs=(anywhere, whole, whole, whole),
+        scratch_shapes=[
+            pltpu.VMEM((2, ROWS, 11 * BLK), jnp.bfloat16),
+            pltpu.VMEM((2, 8, 4, 16, 128), jnp.float32),
+            pltpu.VMEM((N1, 128, 256), jnp.bfloat16),
+            pltpu.VMEM((N1, 128, 256), jnp.bfloat16),
+            pltpu.VMEM((BLK, 128), jnp.float32),
+            pltpu.VMEM((4, 128, 128), jnp.float32),
+            pltpu.VMEM((2, 128, 32, 128), jnp.bfloat16),
+            pltpu.VMEM(taps.shape, taps.dtype),
+            pltpu.VMEM(twist.shape, twist.dtype),
+            pltpu.VMEM(dft.shape, dft.dtype),
+            pltpu.VMEM(flags.shape, flags.dtype),
+            pltpu.VMEM(index.shape, index.dtype),
+            pltpu.VMEM((1024, 128), jnp.float32),
+            pltpu.SemaphoreType.DMA((5,)),
+            pltpu.SemaphoreType.DMA,
+            pltpu.SemaphoreType.DMA,
+            pltpu.SemaphoreType.DMA((3,)),
+            pltpu.SemaphoreType.DMA((3,)),
+            pltpu.SemaphoreType.DMA((2,)),
+            pltpu.SemaphoreType.DMA((2,)),
+        ],
+        compiler_params=pltpu.CompilerParams(
+            vmem_limit_bytes=FIRST_LIMIT, collective_id=0, has_side_effects=True
+        ),
+        cost_estimate=pl.CostEstimate(flops=10**10, bytes_accessed=10**7, transcendentals=0),
+        name="spectra",
+    )(chan_map, voltages, history, taps, twist, dft, flags, index, table)
+
+
+def correlate_kernel(arrived, mask_ref, weight_ref, inverse_ref, vis_ref, power_ref, left, right):
+    later, earlier = arrived.at[0], arrived.at[1]
     step = pl.program_id(0)
     lane = lax.broadcasted_iota(jnp.int32, (256, 128), 1)
     real_lane = lane < 64
@@ -294,7 +402,7 @@
                 total += beam * beam
             total += pltpu.roll(total, 64, 1)
             total += pltpu.roll(total, 32, 1)
-            power_ref[t] = total[:, :32] * 0.125
+            power_ref[t] = (total * 0.125).T[:32]
 
     rows = pl.ds(pl.multiple_of(step * 256, 256), 256)
     inverse = inverse_ref[...]
@@ -304,49 +412,38 @@
             vis_ref[0, t, part] = (value * inverse).astype(jnp.bfloat16)
 
 
-def correlate(later, earlier, mask, weight, inverse):
+def correlate(arrived, mask, weight, inverse):
     return pl.pallas_call(
         correlate_kernel,
         grid=(4,),
         out_shape=(
             jax.ShapeDtypeStruct((1, 2, 2, 1024, 1024), jnp.bfloat16),
-            jax.ShapeDtypeStruct((2, 256, 32), jnp.float32),
+            jax.ShapeDtypeStruct((2, 32, 256), jnp.float32),
         ),
         in_specs=[
-            pl.BlockSpec((4, 1024, 128), lambda i: (0, 0, 0)),
-            pl.BlockSpec((4, 1024, 128), lambda i: (0, 0, 0)),
+            pl.BlockSpec((2, 4, 1024, 128), lambda i: (0, 0, 0, 0)),
             pl.BlockSpec((1024, 128), lambda i: (0, 0)),
             pl.BlockSpec((512, 1024), lambda i: (0, 0)),
             pl.BlockSpec((256, 1024), lambda i: (i, 0)),
         ],
         out_specs=(
             pl.BlockSpec((1, 2, 2, 256, 1024), lambda i: (0, 0, 0, i, 0)),
-            pl.BlockSpec((2, 256, 32), lambda i: (0, 0, 0)),
+            pl.BlockSpec((2, 32, 256), lambda i: (0, 0, 0)),
         ),
         scratch_shapes=[pltpu.VMEM((2, 1024, 512), jnp.bfloat16)] * 2,
         compiler_params=pltpu.CompilerParams(vmem_limit_bytes=VMEM_LIMIT),
         cost_estimate=pl.CostEstimate(flops=6 * 10**9, bytes_accessed=16 * 10**6, transcendentals=0),
         name="correlate",
-    )(later, earlier, mask, weight, inverse)
+    )(arrived, mask, weight, inverse)
 
 
 def per_device(voltages, history, pfb_taps, chan_map, flag_lists, beam_index, beam_table):
-    n_grp = lax.axis_size("grp")
-    n_dev = lax.axis_size("dev")
     twist, dft = tables()
-    after = lax.ppermute(voltages[:, :, :BLK], "grp", [(n, (n - 1) % n_grp) for n in range(n_grp)])
-    before = lax.ppermute(voltages[:, :, 2 * BLK :], "grp", [(n, n + 1) for n in range(n_grp - 1)])
-    line = (chan_map % N1) * N2 + chan_map // N1
-    later = spectra((0, 4), line, voltages, history, after, pfb_taps, twist, dft)
-    later = lax.all_to_all(later, ("grp", "dev"), split_axis=0, concat_axis=0, tiled=True)
-    earlier = spectra((0, 1), line, voltages, history, before, pfb_taps, twist, dft)
-    earlier = lax.all_to_all(earlier, ("grp", "dev"), split_axis=0, concat_axis=0, tiled=True)
-
-    my_bin = lax.axis_index("grp") * n_dev + lax.axis_index("dev")
-    mine = jnp.tile(lax.dynamic_slice_in_dim(chan_map, my_bin * 32, 32), 4)[None, :]
-    table = jnp.pad(beam_table, ((0, 0), (0, 64)))
-    mask, weight, inverse = side(jnp.repeat(flag_lists, 2, axis=0), mine, beam_index, table)
-    return correlate(later.reshape(4, 1024, 128), earlier.reshape(4, 1024, 128), mask, weight, inverse)
+    arrived, mask, weight, inverse = spectra(
+        chan_map, voltages, history, pfb_taps, twist, dft, flag_lists, beam_index, beam_table
+    )
+    visibilities, power = correlate(arrived.reshape(2, 4, 1024, 128), mask, weight, inverse)
+    return visibilities, power.transpose(0, 2, 1)
 
 
 def solution(mesh):

time: 123 us -> 90 us (0.73)
  starting transfers between devices: 28.8 us -> 0 us
  Pallas kernels: 59.8 us -> 83.5 us
  waiting for transfers between devices: 15 us -> 0 us
  local copies, waits for them, and re-layouts: 17 us -> 5.36 us
    pallas_call x3 -> x1, Pallas kernels: 48.4 us -> 72 us  [spectra(): pl.pallas_call(spectra_kernel, out_shape=(jax.ShapeDtypeStruct((2, 128, 3...]
    all_to_all x2 -> x0, starting transfers between devices: 22.9 us -> none  [the longest x1 12 us: per_device(): lax.all_to_all(later, ('grp', 'dev'), split_axis=0, concat_axis=0, tiled=...]
    all_to_all x2 -> x0, waiting for transfers between devices: 9.72 us -> none  [the longest x1 9.72 us: per_device(): lax.all_to_all(earlier, ('grp', 'dev'), split_axis=0, concat_axis=0, tile...]
    unnamed x35 -> x7, local copies, waits for them, and re-layouts: 11.9 us -> 5.36 us
    ppermute x2 -> x0, starting transfers between devices: 5.89 us -> none  [the longest x1 3.63 us: per_device(): lax.ppermute(voltages[:, :, :BLK], 'grp', [(n, (n - 1) % n_grp) for n in...]
    ppermute x2 -> x0, waiting for transfers between devices: 5.31 us -> none  [the longest x1 5.31 us: per_device(): lax.ppermute(voltages[:, :, :BLK], 'grp', [(n, (n - 1) % n_grp) for n in...]
    slice x2 -> x0, local copies, waits for them, and re-layouts: 3.36 us -> none  [the longest x1 2.28 us: per_device(): voltages[:, :, 2 * BLK:]]
  transfers between devices with their start and end apart: 4 -> 0, of which waited for: 2 -> 0; matrix products, arithmetic and copies ran while one was open for 3% -> 0% of each run, Pallas kernels for 40% -> 0%
where the time goes in v1:
time: 90 us; the launch traced here: 89.5 us
  Pallas kernels  83.5 us (93%)
  local copies, waits for them, and re-layouts  5.36 us (6%)
    pallas_call x1, Pallas kernels, spectra(): pl.pallas_call(spectra_kernel, out_shape=(jax.ShapeDtypeStruct((2, 128, 3...  72 us
    pallas_call x1, Pallas kernels, correlate(): pl.pallas_call(correlate_kernel, grid=(4,), out_shape=(jax.ShapeDtypeStru...  11.5 us
    unnamed x7, local copies, waits for them, and re-layouts  5.36 us

profile of v1, /device:TPU:1, one launch (start us, length us, event | category | flops | bytes accessed | tf_op | source)
XLA Modules:
  0.0 89.5 jit_solution(10346809612884880936)
XLA Ops:
  0.6 1.6 %copy.11.flags_hbm = s32[512,12]{1,0:T(8,128)} copy(s32[512,12]{0,1:T(8,128)} %param.13) | data formatting | bytes 49152 | tf_op args[4]
  2.2 72.0 %spectra.1 = (bf16[2,128,32,128]{3,2,1,0:T(8,128)(2,1)}, bf16[1024,128]{1,0:T(8,128)(2,1)}, bf16[512,1024]{1,0:T(8,128)(2,1)}, f32[1024,1024]{1,0:T(8,128)}) custom-call(s32[4096]{0:T(1024)} %chan_ref.1, bf16[2,32,16384]{2,1,0:T(8,128)(2,1)} %own.1, bf16[2,32,12288]{2,1,0:T(8,128)(2,1)} %history.1, f32[4,4096]{1,0:T(4,128)} %taps_hbm.1, ...), custom_call_target="tpu_custom_call" | custom-call | flops 10000000000 | bytes 10000000 | tf_op jit(solution)/shard_map/spectra/pallas_call | solution.py:329
  74.3 0.0 copy-start
  74.3 1.6 %copy-done = bf16[2,128,32,128]{3,2,1,0:T(8,128)(2,1)S(1)} copy-done((bf16[2,128,32,128]{3,2,1,0:T(8,128)(2,1)S(1)}, bf16[2,128,32,128]{3,2,1,0:T(8,128)(2,1)}, u32[]{:S(2)}) %copy-start) | copy-done | bytes 2097176
  75.9 0.0 copy-start.1
  75.9 1.2 %copy-done.1 = bf16[512,1024]{1,0:T(8,128)(2,1)S(1)} copy-done((bf16[512,1024]{1,0:T(8,128)(2,1)S(1)}, bf16[512,1024]{1,0:T(8,128)(2,1)}, u32[]{:S(2)}) %copy-start.1) | copy-done | bytes 1048600
  77.1 0.0 copy-start.2
  77.1 0.9 %copy-done.2 = bf16[1024,128]{1,0:T(8,128)(2,1)S(1)} copy-done((bf16[1024,128]{1,0:T(8,128)(2,1)S(1)}, bf16[1024,128]{1,0:T(8,128)(2,1)}, u32[]{:S(2)}) %copy-start.2) | copy-done | bytes 262168
  78.0 11.5 %correlate.1 = (bf16[1,2,2,1024,1024]{4,3,2,1,0:T(8,128)(2,1)}, f32[2,32,256]{2,1,0:T(8,128)}) custom-call(bf16[2,4,1024,128]{3,2,1,0:T(8,128)(2,1)S(1)} %bitcast.2, bf16[1024,128]{1,0:T(8,128)(2,1)S(1)} %copy-done.2, bf16[512,1024]{1,0:T(8,128)(2,1)S(1)} %copy-done.1, f32[1024,1024]{1,0:T(8,128)} %get-tuple-element.11.inverse_ref), custom_call_target="tpu_custom_call" | custom-call | flops 6000000000 | bytes 16000000 | tf_op jit(solution)/shard_map/correlate/pallas_call | solution.py:416
Async XLA Ops:
  74.3 1.6 %copy-start = (bf16[2,128,32,128]{3,2,1,0:T(8,128)(2,1)S(1)}, bf16[2,128,32,128]{3,2,1,0:T(8,128)(2,1)}, u32[]{:S(2)}) copy-start(bf16[2,128,32,128]{3,2,1,0:T(8,128)(2,1)} %get-tuple-element.8) | copy-start | bytes 6291460
  75.9 1.2 %copy-start.1 = (bf16[512,1024]{1,0:T(8,128)(2,1)S(1)}, bf16[512,1024]{1,0:T(8,128)(2,1)}, u32[]{:S(2)}) copy-start(bf16[512,1024]{1,0:T(8,128)(2,1)} %get-tuple-element.10.weight_ref) | copy-start | bytes 3145732
  77.1 0.9 %copy-start.2 = (bf16[1024,128]{1,0:T(8,128)(2,1)S(1)}, bf16[1024,128]{1,0:T(8,128)(2,1)}, u32[]{:S(2)}) copy-start(bf16[1024,128]{1,0:T(8,128)(2,1)} %get-tuple-element.9.mask_ref) | copy-start | bytes 786436

commit v2 on v1

--- a/solution.py
+++ b/solution.py
@@ -13,8 +13,7 @@
 N2 = 128
 BLK = N1 * N2
 ROWS = 32
-FIRST_LIMIT = 60 * 1024 * 1024
-VMEM_LIMIT = 48 * 1024 * 1024
+VMEM_LIMIT = 60 * 1024 * 1024
 NT = (((1,), (1,)), ((), ()))
 
 
@@ -137,11 +136,12 @@
     mine = jnp.zeros((8, 128), jnp.int32)
     for q in range(32):
         mine = jnp.where(lane == q, chan_ref[my_bin * 32 + q], mine)
-    mine = mine[0:1]
-    flagged = flags_ref[:, 0:1] == mine
-    for n in range(1, flags_ref.shape[1]):
-        flagged = flagged | (flags_ref[:, n : n + 1] == mine)
-    clean = jnp.where(flagged, 0.0, 1.0)
+    mine = jnp.broadcast_to(mine[0:1], (128, 128)).T
+    mine = jnp.concatenate([mine] * (flags_ref.shape[1] // 128), axis=1)
+    flagged = flags_ref[0:1, :] == mine
+    for n in range(1, flags_ref.shape[0]):
+        flagged = flagged | (flags_ref[n : n + 1, :] == mine)
+    clean = jnp.where(flagged, 0.0, 1.0).T
     twice[pl.ds(0, 512, stride=2), :] = clean
     twice[pl.ds(1, 512, stride=2), :] = clean
     mask_ref[...] = twice[...].astype(jnp.bfloat16)
@@ -172,41 +172,52 @@
 
 
 def spectra_kernel(
-    chan_ref, own, history, taps_hbm, twist_hbm, dft_hbm, flags_hbm, index_hbm, table_ref,
-    arrived, mask_ref, weight_ref, inverse_ref,
-    src, mid, high, low, lines, picked, out, taps_ref, twist_ref, dft_ref, flags_ref, index_ref, twice,
-    load_sem, own_sem, rim_sem, halo_send, halo_recv, send_sem, recv_sem,
+    chan_ref, own, history, taps_hbm, twist_hbm, dft_hbm, flags_hbm, index_hbm, table_hbm,
+    arrived, mask_hbm, weight_hbm, inverse_hbm,
+    src, mid, high, low, lines, picked, out, taps_ref, twist_ref, dft_ref, flags_ref, index_ref, table_ref,
+    twice, mask_ref, weight_ref, inverse_ref,
+    load_sem, side_sem, own_sem, rim_sem, halo_send, halo_recv, send_sem, recv_sem,
 ):
     grp, dev = lax.axis_index("grp"), lax.axis_index("dev")
     n_grp, n_dev = lax.axis_size("grp"), lax.axis_size("dev")
     count = n_grp * n_dev
     me = grp * n_dev + dev
-    left, right = lax.rem(grp + n_grp - 1, n_grp), lax.rem(grp + 1, n_grp)
+    planes = [lax.rem(grp + n, n_grp) for n in range(n_grp)]
+    left, right = planes[n_grp - 1], planes[1]
     is_first, is_last = grp == 0, grp == n_grp - 1
     barrier = pltpu.get_barrier_semaphore()
 
-    @pl.loop(1, count)
-    def _(n):
-        peer = lax.rem(me + n, count)
-        pl.semaphore_signal(
-            barrier, inc=1, device_id=(peer // n_dev, lax.rem(peer, n_dev)), device_id_type=pl.DeviceIdType.MESH
-        )
-
-    def blocks(ref, start, number):
-        return ref.at[:, :, pl.ds(pl.multiple_of(start * BLK, BLK), number * BLK)]
-
+    for n in (1, 3, 2, 0):
+
+        @pl.loop(0, n_dev, unroll=8)
+        def _(peer):
+            def greet():
+                pl.semaphore_signal(
+                    barrier, inc=1, device_id=(planes[n], peer), device_id_type=pl.DeviceIdType.MESH
+                )
+
+            if n:
+                greet()
+            else:
+                pl.when(peer != dev)(greet)
+
+    def blocks(ref, start, number, rows=slice(None)):
+        return ref.at[:, rows, pl.ds(pl.multiple_of(start * BLK, BLK), number * BLK)]
+
+    low_rows, high_rows = pl.ds(0, 16), pl.ds(16, 16)
     loads = [
+        pltpu.make_async_copy(own, blocks(src, 2, 4), own_sem),
         pltpu.make_async_copy(taps_hbm, taps_ref, load_sem.at[0]),
         pltpu.make_async_copy(twist_hbm, twist_ref, load_sem.at[1]),
         pltpu.make_async_copy(dft_hbm, dft_ref, load_sem.at[2]),
         pltpu.make_async_copy(flags_hbm, flags_ref, load_sem.at[3]),
         pltpu.make_async_copy(index_hbm, index_ref, load_sem.at[4]),
-        pltpu.make_async_copy(own, blocks(src, 2, 4), own_sem),
+        pltpu.make_async_copy(table_hbm, table_ref, load_sem.at[5]),
     ]
-    for load in reversed(loads):
+    for load in loads:
         load.start()
     rim_first = pltpu.make_async_copy(blocks(history, 1, 2), blocks(src, 0, 2), rim_sem)
-    rim_last = pltpu.make_async_copy(blocks(history, 0, 3), blocks(src, 7, 3), rim_sem)
+    rim_last = pltpu.make_async_copy(blocks(history, 0, 3), blocks(src, 8, 3), rim_sem)
 
     @pl.when(is_first)
     def _():
@@ -216,19 +227,21 @@
     def _():
         rim_last.start()
 
-    def halo(block, at, slot, target):
+    def halo(block, at, rows, slot, target):
         return pltpu.make_async_remote_copy(
-            src_ref=blocks(own, block, 1),
-            dst_ref=blocks(src, at, 1),
+            src_ref=blocks(own, block, 1, rows),
+            dst_ref=blocks(src, at, 1, rows),
             send_sem=halo_send.at[slot],
             recv_sem=halo_recv.at[slot],
             device_id=(target, dev),
             device_id_type=pl.DeviceIdType.MESH,
         )
 
-    after = halo(0, jnp.where(is_first, 10, 6), 0, left)
-    near = halo(3, 1, 1, right)
-    far = halo(2, 0, 2, right)
+    from_right = jnp.where(is_first, 11, 6)
+    after = halo(0, from_right, pl.ds(0, 32), 0, left)
+    beyond = halo(1, from_right + 1, high_rows, 3, left)
+    near = halo(3, 1, pl.ds(0, 32), 1, right)
+    far = halo(2, 0, low_rows, 2, right)
 
     pl.semaphore_wait(barrier, count - 1)
     after.start()
@@ -236,61 +249,78 @@
     @pl.when(jnp.logical_not(is_last))
     def _():
         near.start()
+
+    beyond.start()
+
+    @pl.when(jnp.logical_not(is_last))
+    def _():
         far.start()
 
     for load in loads:
         load.wait()
 
-    def filtered(window, line):
+    def filtered(window, line, row0):
+        first_stage(src, window * BLK, row0, taps_ref, twist_ref, mid, high, low, line + row0)
+
+    def both_halves(window, line):
         @pl.loop(0, ROWS // 16)
         def _(half):
-            row0 = pl.multiple_of(half * 16, 16)
-            first_stage(src, window * BLK, row0, taps_ref, twist_ref, mid, high, low, line + row0)
+            filtered(window, line, pl.multiple_of(half * 16, 16))
 
     def finish(batch):
-        @pl.loop(0, N1 // 4)
+        @pl.loop(0, N1 // 8)
         def _(step):
-            for n in range(4):
-                second_stage(step * 4 + n, dft_ref, high, low, lines)
+            for n in range(8):
+                second_stage(step * 8 + n, dft_ref, high, low, lines)
 
         @pl.loop(0, 8)
         def _(step):
-            at = lax.rem(step + me // 16, 8) * 16
-            for part in range(4):
+            first = lax.rem(step + dev // 4, 8) * 4
+            for part in range(n_grp):
+                at = planes[part] * n_dev + first
                 for n in range(128):
-                    row = chan_ref[(at + part * 4) * 32 + n]
-                    picked[part, pl.ds(n, 1), :] = lines[pl.ds(row, 1), :]
+                    picked[part, pl.ds(n, 1), :] = lines[pl.ds(chan_ref[at * 32 + n], 1), :]
                 for n, block in enumerate(block_turn(picked[part])):
-                    out[batch, at + part * 4 + n] = block.astype(jnp.bfloat16)
-
-            @pl.loop(0, 16)
-            def _(n):
-                peer = at + n
-
-                @pl.when(peer != me)
-                def _():
-                    pltpu.make_async_remote_copy(
-                        src_ref=out.at[batch, peer],
-                        dst_ref=arrived.at[batch, me],
-                        send_sem=send_sem.at[batch],
-                        recv_sem=recv_sem.at[batch],
-                        device_id=(peer // n_dev, lax.rem(peer, n_dev)),
-                        device_id_type=pl.DeviceIdType.MESH,
-                    ).start()
-
-                @pl.when(peer == me)
-                def _():
-                    pltpu.make_async_copy(out.at[batch, me], arrived.at[batch, me], recv_sem.at[batch]).start()
-
-    filtered(2, 0)
+                    out[batch, at + n] = block.astype(jnp.bfloat16)
+            for part in (2, 1, 3, 0):
+                for n in range(4):
+                    peer = first + n
+                    place = planes[part] * n_dev + peer
+
+                    def send():
+                        pltpu.make_async_remote_copy(
+                            src_ref=out.at[batch, place],
+                            dst_ref=arrived.at[batch, me],
+                            send_sem=send_sem.at[batch],
+                            recv_sem=recv_sem.at[batch],
+                            device_id=(planes[part], peer),
+                            device_id_type=pl.DeviceIdType.MESH,
+                        ).start()
+
+                    if part:
+                        send()
+                    else:
+                        pl.when(peer != dev)(send)
+
+        pltpu.make_async_copy(out.at[batch, me], arrived.at[batch, me], recv_sem.at[batch]).start()
+
+    both_halves(2, 0)
     side_work(me, chan_ref, flags_ref, index_ref, table_ref, mask_ref, weight_ref, inverse_ref, twice)
+    side_copies = [
+        pltpu.make_async_copy(held, kept, side_sem.at[n])
+        for n, (held, kept) in enumerate(
+            ((mask_ref, mask_hbm), (weight_ref, weight_hbm), (inverse_ref, inverse_hbm))
+        )
+    ]
+    for copy in side_copies:
+        copy.start()
 
     @pl.when(is_last)
     def _():
         rim_last.wait()
 
     after.wait_recv()
-    filtered(jnp.where(is_last, 7, 3), 32)
+    both_halves(jnp.where(is_last, 8, 3), 32)
     finish(0)
 
     @pl.when(is_first)
@@ -301,97 +331,124 @@
     def _():
         near.wait_recv()
 
-    filtered(1, 32)
+    both_halves(1, 32)
 
     @pl.when(jnp.logical_not(is_first))
     def _():
         far.wait_recv()
 
-    filtered(0, 0)
+    filtered(0, 0, 0)
+    beyond.wait_recv()
+    filtered(jnp.where(is_last, 9, 4), 0, 16)
     finish(1)
 
     after.wait_send()
+    beyond.wait_send()
 
     @pl.when(jnp.logical_not(is_last))
     def _():
         near.wait_send()
         far.wait_send()
 
+    for copy in side_copies:
+        copy.wait()
     for batch in range(2):
         sent = out.at[batch, pl.ds(0, count - 1)]
         pltpu.make_async_copy(sent, sent, send_sem.at[batch]).wait()
         pltpu.make_async_copy(arrived.at[batch], arrived.at[batch], recv_sem.at[batch]).wait()
 
 
-def spectra(chan_map, voltages, history, taps, twist, dft, flags, index, table):
-    whole = pl.BlockSpec(memory_space=pltpu.VMEM)
+def spectra(chan_map, *arrays):
     anywhere = pl.BlockSpec(memory_space=pl.ANY)
+    side = (
+        jax.ShapeDtypeStruct((1024, 128), jnp.bfloat16),
+        jax.ShapeDtypeStruct((512, 1024), jnp.bfloat16),
+        jax.ShapeDtypeStruct((1024, 1024), jnp.float32),
+    )
     return pl.pallas_call(
         spectra_kernel,
-        out_shape=(
-            jax.ShapeDtypeStruct((2, 128, 32, 128), jnp.bfloat16),
-            jax.ShapeDtypeStruct((1024, 128), jnp.bfloat16),
-            jax.ShapeDtypeStruct((512, 1024), jnp.bfloat16),
-            jax.ShapeDtypeStruct((1024, 1024), jnp.float32),
-        ),
-        in_specs=[pl.BlockSpec(memory_space=pltpu.SMEM)] + [anywhere] * 7 + [whole],
-        out_specs=(anywhere, whole, whole, whole),
+        out_shape=(jax.ShapeDtypeStruct((2, 128, 32, 128), jnp.bfloat16),) + side,
+        in_specs=[pl.BlockSpec(memory_space=pltpu.SMEM)] + [anywhere] * len(arrays),
+        out_specs=(anywhere,) * 4,
         scratch_shapes=[
-            pltpu.VMEM((2, ROWS, 11 * BLK), jnp.bfloat16),
+            pltpu.VMEM((2, ROWS, 13 * BLK), jnp.bfloat16),
             pltpu.VMEM((2, 8, 4, 16, 128), jnp.float32),
             pltpu.VMEM((N1, 128, 256), jnp.bfloat16),
             pltpu.VMEM((N1, 128, 256), jnp.bfloat16),
             pltpu.VMEM((BLK, 128), jnp.float32),
             pltpu.VMEM((4, 128, 128), jnp.float32),
             pltpu.VMEM((2, 128, 32, 128), jnp.bfloat16),
-            pltpu.VMEM(taps.shape, taps.dtype),
-            pltpu.VMEM(twist.shape, twist.dtype),
-            pltpu.VMEM(dft.shape, dft.dtype),
-            pltpu.VMEM(flags.shape, flags.dtype),
-            pltpu.VMEM(index.shape, index.dtype),
-            pltpu.VMEM((1024, 128), jnp.float32),
-            pltpu.SemaphoreType.DMA((5,)),
+        ]
+        + [pltpu.VMEM(array.shape, array.dtype) for array in arrays[2:]]
+        + [pltpu.VMEM((1024, 128), jnp.float32)]
+        + [pltpu.VMEM(result.shape, result.dtype) for result in side]
+        + [
+            pltpu.SemaphoreType.DMA((6,)),
+            pltpu.SemaphoreType.DMA((3,)),
             pltpu.SemaphoreType.DMA,
             pltpu.SemaphoreType.DMA,
-            pltpu.SemaphoreType.DMA((3,)),
-            pltpu.SemaphoreType.DMA((3,)),
+            pltpu.SemaphoreType.DMA((4,)),
+            pltpu.SemaphoreType.DMA((4,)),
             pltpu.SemaphoreType.DMA((2,)),
             pltpu.SemaphoreType.DMA((2,)),
         ],
         compiler_params=pltpu.CompilerParams(
-            vmem_limit_bytes=FIRST_LIMIT, collective_id=0, has_side_effects=True
+            vmem_limit_bytes=VMEM_LIMIT, collective_id=0, has_side_effects=True
         ),
         cost_estimate=pl.CostEstimate(flops=10**10, bytes_accessed=10**7, transcendentals=0),
         name="spectra",
-    )(chan_map, voltages, history, taps, twist, dft, flags, index, table)
-
-
-def correlate_kernel(arrived, mask_ref, weight_ref, inverse_ref, vis_ref, power_ref, left, right):
-    later, earlier = arrived.at[0], arrived.at[1]
+    )(chan_map, *arrays)
+
+
+def correlate_kernel(arrived_hbm, mask_hbm, weight_hbm, inverse_ref, vis_ref, power_ref, arrived, mask_ref, weight_ref, left, right, sems):
     step = pl.program_id(0)
     lane = lax.broadcasted_iota(jnp.int32, (256, 128), 1)
+    row = lax.broadcasted_iota(jnp.int32, (256, 128), 0)
     real_lane = lane < 64
+    first = (lane & 32) == 0
+    moved = first & ((row & 16) != 0)
+    load_mask = pltpu.make_async_copy(mask_hbm, mask_ref, sems.at[4])
+    load_weight = pltpu.make_async_copy(weight_hbm, weight_ref, sems.at[5])
+
+    def load_rows(n):
+        rows = pl.ds(n * 256, 256)
+        return pltpu.make_async_copy(arrived_hbm.at[:, :, rows], arrived.at[:, :, rows], sems.at[n])
 
     @pl.when(step == 0)
     def _():
-        @pl.loop(0, 4)
-        def _(n):
-            rows = pl.ds(pl.multiple_of(n * 256, 256), 256)
+        load_mask.start()
+        for n in range(4):
+            load_rows(n).start()
+        load_weight.start()
+        load_mask.wait()
+        for n in range(4):
+            load_rows(n).wait()
+            rows = pl.ds(n * 256, 256)
             mask = mask_ref[rows, :].astype(jnp.float32)
-            first = (lane & 32) == 0
-            one = later[1, rows, :].astype(jnp.float32)
-            three = later[3, rows, :].astype(jnp.float32)
+            late = [arrived[0, g, rows, :].astype(jnp.float32) for g in range(4)]
+            early = [arrived[1, g, rows, :].astype(jnp.float32) for g in range(4)]
+            early = [jnp.where(moved, early[(g + 3) % 4], early[g]) for g in range(4)]
             blocks = (
-                (later[0, rows, :], earlier[0, rows, :], earlier[1, rows, :], jnp.where(first, one, three)),
-                (later[2, rows, :], earlier[2, rows, :], earlier[3, rows, :], jnp.where(first, three, one)),
+                (late[0], early[0], early[1], jnp.where(first, late[1], late[3])),
+                (late[2], early[2], early[3], jnp.where(first, late[3], late[1])),
             )
             for t in range(2):
                 for b in range(4):
-                    masked = blocks[t][b].astype(jnp.float32) * mask
+                    masked = blocks[t][b] * mask
                     crossed = pltpu.roll(masked, 64, 1)
                     left[t, rows, pl.ds(b * 128, 128)] = masked.astype(jnp.bfloat16)
                     right[t, rows, pl.ds(b * 128, 128)] = jnp.where(real_lane, crossed, -crossed).astype(jnp.bfloat16)
 
+    rows = pl.ds(pl.multiple_of(step * 256, 256), 256)
+    inverse = inverse_ref[...]
+    for t in range(2):
+        for part, lhs in enumerate((left, right)):
+            value = lax.dot_general(lhs[t, rows, :], left[t], NT, preferred_element_type=jnp.float32)
+            vis_ref[0, t, part] = (value * inverse).astype(jnp.bfloat16)
+
+    @pl.when(step == 1)
+    def _():
+        load_weight.wait()
         for t in range(2):
             total = jnp.zeros((256, 128), jnp.float32)
             product = jnp.dot(weight_ref[...], left[t], preferred_element_type=jnp.float32)
@@ -404,15 +461,9 @@
             total += pltpu.roll(total, 32, 1)
             power_ref[t] = (total * 0.125).T[:32]
 
-    rows = pl.ds(pl.multiple_of(step * 256, 256), 256)
-    inverse = inverse_ref[...]
-    for t in range(2):
-        for part, lhs in enumerate((left, right)):
-            value = lax.dot_general(lhs[t, rows, :], left[t], NT, preferred_element_type=jnp.float32)
-            vis_ref[0, t, part] = (value * inverse).astype(jnp.bfloat16)
-
 
 def correlate(arrived, mask, weight, inverse):
+    anywhere = pl.BlockSpec(memory_space=pl.ANY)
     return pl.pallas_call(
         correlate_kernel,
         grid=(4,),
@@ -420,17 +471,19 @@
             jax.ShapeDtypeStruct((1, 2, 2, 1024, 1024), jnp.bfloat16),
             jax.ShapeDtypeStruct((2, 32, 256), jnp.float32),
         ),
-        in_specs=[
-            pl.BlockSpec((2, 4, 1024, 128), lambda i: (0, 0, 0, 0)),
-            pl.BlockSpec((1024, 128), lambda i: (0, 0)),
-            pl.BlockSpec((512, 1024), lambda i: (0, 0)),
-            pl.BlockSpec((256, 1024), lambda i: (i, 0)),
-        ],
+        in_specs=[anywhere, anywhere, anywhere, pl.BlockSpec((256, 1024), lambda i: (i, 0))],
         out_specs=(
             pl.BlockSpec((1, 2, 2, 256, 1024), lambda i: (0, 0, 0, i, 0)),
             pl.BlockSpec((2, 32, 256), lambda i: (0, 0, 0)),
         ),
-        scratch_shapes=[pltpu.VMEM((2, 1024, 512), jnp.bfloat16)] * 2,
+        scratch_shapes=[
+            pltpu.VMEM(arrived.shape, jnp.bfloat16),
+            pltpu.VMEM(mask.shape, jnp.bfloat16),
+            pltpu.VMEM(weight.shape, jnp.bfloat16),
+            pltpu.VMEM((2, 1024, 512), jnp.bfloat16),
+            pltpu.VMEM((2, 1024, 512), jnp.bfloat16),
+            pltpu.SemaphoreType.DMA((6,)),
+        ],
         compiler_params=pltpu.CompilerParams(vmem_limit_bytes=VMEM_LIMIT),
         cost_estimate=pl.CostEstimate(flops=6 * 10**9, bytes_accessed=16 * 10**6, transcendentals=0),
         name="correlate",
@@ -440,7 +493,7 @@
 def per_device(voltages, history, pfb_taps, chan_map, flag_lists, beam_index, beam_table):
     twist, dft = tables()
     arrived, mask, weight, inverse = spectra(
-        chan_map, voltages, history, pfb_taps, twist, dft, flag_lists, beam_index, beam_table
+        chan_map, voltages, history, pfb_taps, twist, dft, flag_lists.T, beam_index, beam_table
     )
     visibilities, power = correlate(arrived.reshape(2, 4, 1024, 128), mask, weight, inverse)
     return visibilities, power.transpose(0, 2, 1)

time: 90 us -> 72.8 us (0.81)
  Pallas kernels: 83.5 us -> 71.9 us
  local copies, waits for them, and re-layouts: 5.36 us -> 0 us
    pallas_call x1, Pallas kernels: 72 us -> 59.2 us  [spectra(): pl.pallas_call(spectra_kernel, out_shape=(jax.ShapeDtypeStruct((2, 128, 3...]
    unnamed x7 -> x0, local copies, waits for them, and re-layouts: 5.36 us -> none
    pallas_call x1, Pallas kernels: 11.5 us -> 12.7 us  [correlate(): pl.pallas_call(correlate_kernel, grid=(4,), out_shape=(jax.ShapeDtypeStru...]
where the time goes in v2:
time: 72.8 us; the launch traced here: 72.6 us
  Pallas kernels  71.9 us (99%)
    pallas_call x1, Pallas kernels, spectra(): pl.pallas_call(spectra_kernel, out_shape=(jax.ShapeDtypeStruct((2, 128, 3...  59.2 us
    pallas_call x1, Pallas kernels, correlate(): pl.pallas_call(correlate_kernel, grid=(4,), out_shape=(jax.ShapeDtypeStru...  12.7 us

profile of v2, /device:TPU:1, one launch (start us, length us, event | category | flops | bytes accessed | tf_op | source)
XLA Modules:
  0.0 72.6 jit_solution(18161445068081566270)
XLA Ops:
  0.6 59.2 %spectra.1 = (bf16[2,128,32,128]{3,2,1,0:T(8,128)(2,1)}, bf16[1024,128]{1,0:T(8,128)(2,1)}, bf16[512,1024]{1,0:T(8,128)(2,1)}, f32[1024,1024]{1,0:T(8,128)}) custom-call(s32[4096]{0:T(1024)} %chan_ref.1, bf16[2,32,16384]{2,1,0:T(8,128)(2,1)} %own.1, bf16[2,32,12288]{2,1,0:T(8,128)(2,1)} %history.1, f32[4,4096]{1,0:T(4,128)} %taps_hbm.1, ...), custom_call_target="tpu_custom_call" | custom-call | flops 10000000000 | bytes 10000000 | tf_op jit(solution)/shard_map/spectra/pallas_call | solution.py:368
  59.8 12.7 %correlate.1 = (bf16[1,2,2,1024,1024]{4,3,2,1,0:T(8,128)(2,1)}, f32[2,32,256]{2,1,0:T(8,128)}) custom-call(bf16[2,4,1024,128]{3,2,1,0:T(8,128)(2,1)} %bitcast.4, bf16[1024,128]{1,0:T(8,128)(2,1)} %get-tuple-element.9.mask_hbm, bf16[512,1024]{1,0:T(8,128)(2,1)} %get-tuple-element.10.weight_hbm, f32[1024,1024]{1,0:T(8,128)} %get-tuple-element.11.inverse_ref), custom_call_target="tpu_custom_call" | custom-call | flops 6000000000 | bytes 16000000 | tf_op jit(solution)/shard_map/correlate/pallas_call | solution.py:467

commit v3 on v2

--- a/solution.py
+++ b/solution.py
@@ -13,7 +13,7 @@
 N2 = 128
 BLK = N1 * N2
 ROWS = 32
-VMEM_LIMIT = 60 * 1024 * 1024
+VMEM_LIMIT = 48 * 1024 * 1024
 NT = (((1,), (1,)), ((), ()))
 
 
@@ -173,10 +173,10 @@
 
 def spectra_kernel(
     chan_ref, own, history, taps_hbm, twist_hbm, dft_hbm, flags_hbm, index_hbm, table_hbm,
-    arrived, mask_hbm, weight_hbm, inverse_hbm,
+    vis_ref, power_ref,
     src, mid, high, low, lines, picked, out, taps_ref, twist_ref, dft_ref, flags_ref, index_ref, table_ref,
-    twice, mask_ref, weight_ref, inverse_ref,
-    load_sem, side_sem, own_sem, rim_sem, halo_send, halo_recv, send_sem, recv_sem,
+    twice, mask_ref, weight_ref, inverse_ref, arrived, lefts, rights, partial, beam_sum,
+    load_sem, own_sem, rim_sem, halo_send, halo_recv, send_sem, recv_sem,
 ):
     grp, dev = lax.axis_index("grp"), lax.axis_index("dev")
     n_grp, n_dev = lax.axis_size("grp"), lax.axis_size("dev")
@@ -306,14 +306,6 @@
 
     both_halves(2, 0)
     side_work(me, chan_ref, flags_ref, index_ref, table_ref, mask_ref, weight_ref, inverse_ref, twice)
-    side_copies = [
-        pltpu.make_async_copy(held, kept, side_sem.at[n])
-        for n, (held, kept) in enumerate(
-            ((mask_ref, mask_hbm), (weight_ref, weight_hbm), (inverse_ref, inverse_hbm))
-        )
-    ]
-    for copy in side_copies:
-        copy.start()
 
     @pl.when(is_last)
     def _():
@@ -342,6 +334,24 @@
     filtered(jnp.where(is_last, 9, 4), 0, 16)
     finish(1)
 
+    sent = [out.at[batch, pl.ds(0, count - 1)] for batch in range(2)]
+    for batch in range(2):
+        pltpu.make_async_copy(arrived.at[batch], arrived.at[batch], recv_sem.at[batch]).wait()
+        build(batch, arrived, mask_ref, lefts, rights)
+        beam_share(batch, weight_ref, lefts, power_ref, beam_sum)
+
+        @pl.loop(0, 4)
+        def _(step):
+            rows = pl.ds(pl.multiple_of(step * 256, 256), 256)
+            for t in range(2):
+                for part, lhs in enumerate((lefts, rights)):
+                    value = lax.dot_general(lhs[t, rows, :], lefts[t], NT, preferred_element_type=jnp.float32)
+                    if batch == 0:
+                        partial[t, part, rows, :] = value
+                    else:
+                        value = (value + partial[t, part, rows, :]) * inverse_ref[rows, :]
+                        vis_ref[0, t, part, rows, :] = value.astype(jnp.bfloat16)
+
     after.wait_send()
     beyond.wait_send()
 
@@ -350,26 +360,59 @@
         near.wait_send()
         far.wait_send()
 
-    for copy in side_copies:
-        copy.wait()
     for batch in range(2):
-        sent = out.at[batch, pl.ds(0, count - 1)]
-        pltpu.make_async_copy(sent, sent, send_sem.at[batch]).wait()
-        pltpu.make_async_copy(arrived.at[batch], arrived.at[batch], recv_sem.at[batch]).wait()
+        pltpu.make_async_copy(sent[batch], sent[batch], send_sem.at[batch]).wait()
+
+
+def build(batch, arrived, mask_ref, lefts, rights):
+    lane = lax.broadcasted_iota(jnp.int32, (256, 128), 1)
+    row = lax.broadcasted_iota(jnp.int32, (256, 128), 0)
+    first = (lane & 32) == 0
+    moved = first & ((row & 16) != 0)
+
+    @pl.loop(0, 4)
+    def _(n):
+        rows = pl.ds(pl.multiple_of(n * 256, 256), 256)
+        mask = mask_ref[rows, :].astype(jnp.float32)
+        held = [arrived[batch, pl.ds(g * 32 + n * 8, 8)].reshape(256, 128).astype(jnp.float32) for g in range(4)]
+        if batch == 0:
+            held = [held[0], jnp.where(first, held[1], held[3]), held[2], jnp.where(first, held[3], held[1])]
+        else:
+            held = [jnp.where(moved, held[(g + 3) % 4], held[g]) for g in range(4)]
+        for g in range(4):
+            masked = held[g] * mask
+            crossed = pltpu.roll(masked, 64, 1)
+            lanes = pl.ds(g % 2 * 128, 128)
+            lefts[g // 2, rows, lanes] = masked.astype(jnp.bfloat16)
+            rights[g // 2, rows, lanes] = jnp.where(lane < 64, crossed, -crossed).astype(jnp.bfloat16)
+
+
+def beam_share(batch, weight_ref, lefts, power_ref, beam_sum):
+    real_lane = lax.broadcasted_iota(jnp.int32, (256, 128), 1) < 64
+    for t in range(2):
+        product = jnp.dot(weight_ref[...], lefts[t], preferred_element_type=jnp.float32)
+        total = beam_sum[t] if batch else jnp.zeros((256, 128), jnp.float32)
+        for b in range(2):
+            by_real = product[:256, b * 128 : b * 128 + 128]
+            by_imag = pltpu.roll(product[256:, b * 128 : b * 128 + 128], 64, 1)
+            beam = by_real + jnp.where(real_lane, -by_imag, by_imag)
+            total += beam * beam
+        if batch == 0:
+            beam_sum[t] = total
+        else:
+            total += pltpu.roll(total, 64, 1)
+            total += pltpu.roll(total, 32, 1)
+            power_ref[t] = (total * 0.125).T[:32]
 
 
 def spectra(chan_map, *arrays):
     anywhere = pl.BlockSpec(memory_space=pl.ANY)
-    side = (
-        jax.ShapeDtypeStruct((1024, 128), jnp.bfloat16),
-        jax.ShapeDtypeStruct((512, 1024), jnp.bfloat16),
-        jax.ShapeDtypeStruct((1024, 1024), jnp.float32),
-    )
+    whole = pl.BlockSpec(memory_space=pltpu.VMEM)
     return pl.pallas_call(
         spectra_kernel,
-        out_shape=(jax.ShapeDtypeStruct((2, 128, 32, 128), jnp.bfloat16),) + side,
+        out_shape=(pltpu.VMEM((1, 2, 2, 1024, 1024), jnp.bfloat16), pltpu.VMEM((2, 32, 256), jnp.float32)),
         in_specs=[pl.BlockSpec(memory_space=pltpu.SMEM)] + [anywhere] * len(arrays),
-        out_specs=(anywhere,) * 4,
+        out_specs=(whole, whole),
         scratch_shapes=[
             pltpu.VMEM((2, ROWS, 13 * BLK), jnp.bfloat16),
             pltpu.VMEM((2, 8, 4, 16, 128), jnp.float32),
@@ -380,11 +423,17 @@
             pltpu.VMEM((2, 128, 32, 128), jnp.bfloat16),
         ]
         + [pltpu.VMEM(array.shape, array.dtype) for array in arrays[2:]]
-        + [pltpu.VMEM((1024, 128), jnp.float32)]
-        + [pltpu.VMEM(result.shape, result.dtype) for result in side]
         + [
+            pltpu.VMEM((1024, 128), jnp.float32),
+            pltpu.VMEM((1024, 128), jnp.bfloat16),
+            pltpu.VMEM((512, 1024), jnp.bfloat16),
+            pltpu.VMEM((1024, 1024), jnp.float32),
+            pltpu.VMEM((2, 128, 32, 128), jnp.bfloat16),
+            pltpu.VMEM((2, 1024, 256), jnp.bfloat16),
+            pltpu.VMEM((2, 1024, 256), jnp.bfloat16),
+            pltpu.VMEM((2, 2, 1024, 1024), jnp.float32),
+            pltpu.VMEM((2, 256, 128), jnp.float32),
             pltpu.SemaphoreType.DMA((6,)),
-            pltpu.SemaphoreType.DMA((3,)),
             pltpu.SemaphoreType.DMA,
             pltpu.SemaphoreType.DMA,
             pltpu.SemaphoreType.DMA((4,)),
@@ -400,102 +449,11 @@
     )(chan_map, *arrays)
 
 
-def correlate_kernel(arrived_hbm, mask_hbm, weight_hbm, inverse_ref, vis_ref, power_ref, arrived, mask_ref, weight_ref, left, right, sems):
-    step = pl.program_id(0)
-    lane = lax.broadcasted_iota(jnp.int32, (256, 128), 1)
-    row = lax.broadcasted_iota(jnp.int32, (256, 128), 0)
-    real_lane = lane < 64
-    first = (lane & 32) == 0
-    moved = first & ((row & 16) != 0)
-    load_mask = pltpu.make_async_copy(mask_hbm, mask_ref, sems.at[4])
-    load_weight = pltpu.make_async_copy(weight_hbm, weight_ref, sems.at[5])
-
-    def load_rows(n):
-        rows = pl.ds(n * 256, 256)
-        return pltpu.make_async_copy(arrived_hbm.at[:, :, rows], arrived.at[:, :, rows], sems.at[n])
-
-    @pl.when(step == 0)
-    def _():
-        load_mask.start()
-        for n in range(4):
-            load_rows(n).start()
-        load_weight.start()
-        load_mask.wait()
-        for n in range(4):
-            load_rows(n).wait()
-            rows = pl.ds(n * 256, 256)
-            mask = mask_ref[rows, :].astype(jnp.float32)
-            late = [arrived[0, g, rows, :].astype(jnp.float32) for g in range(4)]
-            early = [arrived[1, g, rows, :].astype(jnp.float32) for g in range(4)]
-            early = [jnp.where(moved, early[(g + 3) % 4], early[g]) for g in range(4)]
-            blocks = (
-                (late[0], early[0], early[1], jnp.where(first, late[1], late[3])),
-                (late[2], early[2], early[3], jnp.where(first, late[3], late[1])),
-            )
-            for t in range(2):
-                for b in range(4):
-                    masked = blocks[t][b] * mask
-                    crossed = pltpu.roll(masked, 64, 1)
-                    left[t, rows, pl.ds(b * 128, 128)] = masked.astype(jnp.bfloat16)
-                    right[t, rows, pl.ds(b * 128, 128)] = jnp.where(real_lane, crossed, -crossed).astype(jnp.bfloat16)
-
-    rows = pl.ds(pl.multiple_of(step * 256, 256), 256)
-    inverse = inverse_ref[...]
-    for t in range(2):
-        for part, lhs in enumerate((left, right)):
-            value = lax.dot_general(lhs[t, rows, :], left[t], NT, preferred_element_type=jnp.float32)
-            vis_ref[0, t, part] = (value * inverse).astype(jnp.bfloat16)
-
-    @pl.when(step == 1)
-    def _():
-        load_weight.wait()
-        for t in range(2):
-            total = jnp.zeros((256, 128), jnp.float32)
-            product = jnp.dot(weight_ref[...], left[t], preferred_element_type=jnp.float32)
-            for b in range(4):
-                by_real = product[:256, b * 128 : b * 128 + 128]
-                by_imag = pltpu.roll(product[256:, b * 128 : b * 128 + 128], 64, 1)
-                beam = by_real + jnp.where(real_lane, -by_imag, by_imag)
-                total += beam * beam
-            total += pltpu.roll(total, 64, 1)
-            total += pltpu.roll(total, 32, 1)
-            power_ref[t] = (total * 0.125).T[:32]
-
-
-def correlate(arrived, mask, weight, inverse):
-    anywhere = pl.BlockSpec(memory_space=pl.ANY)
-    return pl.pallas_call(
-        correlate_kernel,
-        grid=(4,),
-        out_shape=(
-            jax.ShapeDtypeStruct((1, 2, 2, 1024, 1024), jnp.bfloat16),
-            jax.ShapeDtypeStruct((2, 32, 256), jnp.float32),
-        ),
-        in_specs=[anywhere, anywhere, anywhere, pl.BlockSpec((256, 1024), lambda i: (i, 0))],
-        out_specs=(
-            pl.BlockSpec((1, 2, 2, 256, 1024), lambda i: (0, 0, 0, i, 0)),
-            pl.BlockSpec((2, 32, 256), lambda i: (0, 0, 0)),
-        ),
-        scratch_shapes=[
-            pltpu.VMEM(arrived.shape, jnp.bfloat16),
-            pltpu.VMEM(mask.shape, jnp.bfloat16),
-            pltpu.VMEM(weight.shape, jnp.bfloat16),
-            pltpu.VMEM((2, 1024, 512), jnp.bfloat16),
-            pltpu.VMEM((2, 1024, 512), jnp.bfloat16),
-            pltpu.SemaphoreType.DMA((6,)),
-        ],
-        compiler_params=pltpu.CompilerParams(vmem_limit_bytes=VMEM_LIMIT),
-        cost_estimate=pl.CostEstimate(flops=6 * 10**9, bytes_accessed=16 * 10**6, transcendentals=0),
-        name="correlate",
-    )(arrived, mask, weight, inverse)
-
-
 def per_device(voltages, history, pfb_taps, chan_map, flag_lists, beam_index, beam_table):
     twist, dft = tables()
-    arrived, mask, weight, inverse = spectra(
+    visibilities, power = spectra(
         chan_map, voltages, history, pfb_taps, twist, dft, flag_lists.T, beam_index, beam_table
     )
-    visibilities, power = correlate(arrived.reshape(2, 4, 1024, 128), mask, weight, inverse)
     return visibilities, power.transpose(0, 2, 1)
 
 

time: 72.8 us -> 68.6 us (0.942)
  Pallas kernels: 71.9 us -> 63.8 us
  local copies, waits for them, and re-layouts: 0 us -> 4.03 us
    pallas_call x2 -> x1, Pallas kernels: 71.9 us -> 63.8 us  [spectra(): pl.pallas_call(spectra_kernel, out_shape=(pltpu.VMEM((1, 2, 2, 1024, 1024...]
    unnamed x0 -> x2, local copies, waits for them, and re-layouts: none -> 4.03 us
where the time goes in v3:
time: 68.6 us; the launch traced here: 68.5 us
  Pallas kernels  63.8 us (93%)
  local copies, waits for them, and re-layouts  4.03 us (6%)
    pallas_call x1, Pallas kernels, spectra(): pl.pallas_call(spectra_kernel, out_shape=(pltpu.VMEM((1, 2, 2, 1024, 1024...  63.8 us
    unnamed x2, local copies, waits for them, and re-layouts  4.03 us

profile of v3, /device:TPU:1, one launch (start us, length us, event | category | flops | bytes accessed | tf_op | source)
XLA Modules:
  0.0 68.5 jit_solution(10486499602366701860)
XLA Ops:
  0.6 63.8 %spectra.1 = (bf16[1,2,2,1024,1024]{4,3,2,1,0:T(8,128)(2,1)S(1)}, f32[2,32,256]{2,1,0:T(8,128)S(1)}) custom-call(s32[4096]{0:T(1024)} %chan_ref.1, bf16[2,32,16384]{2,1,0:T(8,128)(2,1)} %own.1, bf16[2,32,12288]{2,1,0:T(8,128)(2,1)} %history.1, f32[4,4096]{1,0:T(4,128)} %taps_hbm.1, f32[2,32,128]{2,1,0:T(8,128)} %constant.4.clone.twist_hbm, ...), custom_call_target="tpu_custom_call" | custom-call | flops 10000000000 | bytes 10000000 | tf_op jit(solution)/shard_map/spectra/pallas_call | solution.py:411
  64.4 3.4 %copy.13 = bf16[1,2,2,1024,1024]{4,3,2,1,0:T(8,128)(2,1)} copy(bf16[1,2,2,1024,1024]{4,3,2,1,0:T(8,128)(2,1)S(1)} %get-tuple-element.6) | data formatting | bytes 16777216
  67.8 0.6 copy.14

commit v4 on v3

--- a/solution.py
+++ b/solution.py
@@ -13,7 +13,8 @@
 N2 = 128
 BLK = N1 * N2
 ROWS = 32
-VMEM_LIMIT = 48 * 1024 * 1024
+FIRST_LIMIT = 32 * 1024 * 1024
+LAST_LIMIT = 24 * 1024 * 1024
 NT = (((1,), (1,)), ((), ()))
 
 
@@ -173,9 +174,9 @@
 
 def spectra_kernel(
     chan_ref, own, history, taps_hbm, twist_hbm, dft_hbm, flags_hbm, index_hbm, table_hbm,
-    vis_ref, power_ref,
+    lefts, rights, inverse_ref, weight_ref, beam_sum, part0, part1, part2, part3,
     src, mid, high, low, lines, picked, out, taps_ref, twist_ref, dft_ref, flags_ref, index_ref, table_ref,
-    twice, mask_ref, weight_ref, inverse_ref, arrived, lefts, rights, partial, beam_sum,
+    twice, mask_ref, arrived,
     load_sem, own_sem, rim_sem, halo_send, halo_recv, send_sem, recv_sem,
 ):
     grp, dev = lax.axis_index("grp"), lax.axis_index("dev")
@@ -267,7 +268,7 @@
         def _(half):
             filtered(window, line, pl.multiple_of(half * 16, 16))
 
-    def finish(batch):
+    def send_batch(batch):
         @pl.loop(0, N1 // 8)
         def _(step):
             for n in range(8):
@@ -275,16 +276,16 @@
 
         @pl.loop(0, 8)
         def _(step):
-            first = lax.rem(step + dev // 4, 8) * 4
-            for part in range(n_grp):
+            firsts = [lax.rem(step + dev // 4 + turn, 8) * 4 for turn in (0, 3, 4, 7)]
+            for part, first in enumerate(firsts):
                 at = planes[part] * n_dev + first
                 for n in range(128):
                     picked[part, pl.ds(n, 1), :] = lines[pl.ds(chan_ref[at * 32 + n], 1), :]
                 for n, block in enumerate(block_turn(picked[part])):
                     out[batch, at + n] = block.astype(jnp.bfloat16)
-            for part in (2, 1, 3, 0):
-                for n in range(4):
-                    peer = first + n
+            for n in range(4):
+                for part in (2, 1, 3, 0):
+                    peer = firsts[part] + n
                     place = planes[part] * n_dev + peer
 
                     def send():
@@ -313,7 +314,7 @@
 
     after.wait_recv()
     both_halves(jnp.where(is_last, 8, 3), 32)
-    finish(0)
+    send_batch(0)
 
     @pl.when(is_first)
     def _():
@@ -332,26 +333,21 @@
     filtered(0, 0, 0)
     beyond.wait_recv()
     filtered(jnp.where(is_last, 9, 4), 0, 16)
-    finish(1)
-
-    sent = [out.at[batch, pl.ds(0, count - 1)] for batch in range(2)]
-    for batch in range(2):
-        pltpu.make_async_copy(arrived.at[batch], arrived.at[batch], recv_sem.at[batch]).wait()
-        build(batch, arrived, mask_ref, lefts, rights)
-        beam_share(batch, weight_ref, lefts, power_ref, beam_sum)
-
-        @pl.loop(0, 4)
-        def _(step):
-            rows = pl.ds(pl.multiple_of(step * 256, 256), 256)
-            for t in range(2):
-                for part, lhs in enumerate((lefts, rights)):
-                    value = lax.dot_general(lhs[t, rows, :], lefts[t], NT, preferred_element_type=jnp.float32)
-                    if batch == 0:
-                        partial[t, part, rows, :] = value
-                    else:
-                        value = (value + partial[t, part, rows, :]) * inverse_ref[rows, :]
-                        vis_ref[0, t, part, rows, :] = value.astype(jnp.bfloat16)
-
+    send_batch(1)
+
+    pltpu.make_async_copy(arrived.at[0], arrived.at[0], recv_sem.at[0]).wait()
+    build(0, arrived, mask_ref, lefts, rights)
+
+    @pl.loop(0, 4)
+    def _(step):
+        rows = pl.ds(pl.multiple_of(step * 256, 256), 256)
+        for t in range(2):
+            for part, lhs in enumerate((lefts, rights)):
+                (part0, part1, part2, part3)[2 * t + part][rows, :] = lax.dot_general(
+                    lhs[t, rows, :], lefts[t], NT, preferred_element_type=jnp.float32
+                )
+
+    beam_share(weight_ref, lefts, beam_sum)
     after.wait_send()
     beyond.wait_send()
 
@@ -361,7 +357,10 @@
         far.wait_send()
 
     for batch in range(2):
-        pltpu.make_async_copy(sent[batch], sent[batch], send_sem.at[batch]).wait()
+        sent = out.at[batch, pl.ds(0, count - 1)]
+        pltpu.make_async_copy(sent, sent, send_sem.at[batch]).wait()
+    pltpu.make_async_copy(arrived.at[1], arrived.at[1], recv_sem.at[1]).wait()
+    build(1, arrived, mask_ref, lefts, rights)
 
 
 def build(batch, arrived, mask_ref, lefts, rights):
@@ -387,22 +386,23 @@
             rights[g // 2, rows, lanes] = jnp.where(lane < 64, crossed, -crossed).astype(jnp.bfloat16)
 
 
-def beam_share(batch, weight_ref, lefts, power_ref, beam_sum):
+def beam_share(weight_ref, lefts, beam_sum, before=None):
     real_lane = lax.broadcasted_iota(jnp.int32, (256, 128), 1) < 64
     for t in range(2):
         product = jnp.dot(weight_ref[...], lefts[t], preferred_element_type=jnp.float32)
-        total = beam_sum[t] if batch else jnp.zeros((256, 128), jnp.float32)
+        total = jnp.zeros((256, 128), jnp.float32)
         for b in range(2):
             by_real = product[:256, b * 128 : b * 128 + 128]
             by_imag = pltpu.roll(product[256:, b * 128 : b * 128 + 128], 64, 1)
             beam = by_real + jnp.where(real_lane, -by_imag, by_imag)
             total += beam * beam
-        if batch == 0:
+        if before is None:
             beam_sum[t] = total
         else:
+            total += before[t]
             total += pltpu.roll(total, 64, 1)
             total += pltpu.roll(total, 32, 1)
-            power_ref[t] = (total * 0.125).T[:32]
+            beam_sum[t] = (total * 0.125).T[:32]
 
 
 def spectra(chan_map, *arrays):
@@ -410,9 +410,16 @@
     whole = pl.BlockSpec(memory_space=pltpu.VMEM)
     return pl.pallas_call(
         spectra_kernel,
-        out_shape=(pltpu.VMEM((1, 2, 2, 1024, 1024), jnp.bfloat16), pltpu.VMEM((2, 32, 256), jnp.float32)),
+        out_shape=(
+            pltpu.VMEM((2, 1024, 256), jnp.bfloat16),
+            pltpu.VMEM((2, 1024, 256), jnp.bfloat16),
+            pltpu.VMEM((1024, 1024), jnp.float32),
+            pltpu.VMEM((512, 1024), jnp.bfloat16),
+            pltpu.VMEM((2, 256, 128), jnp.float32),
+        )
+        + (pltpu.VMEM((1024, 1024), jnp.float32),) * 4,
         in_specs=[pl.BlockSpec(memory_space=pltpu.SMEM)] + [anywhere] * len(arrays),
-        out_specs=(whole, whole),
+        out_specs=(whole,) * 9,
         scratch_shapes=[
             pltpu.VMEM((2, ROWS, 13 * BLK), jnp.bfloat16),
             pltpu.VMEM((2, 8, 4, 16, 128), jnp.float32),
@@ -426,13 +433,7 @@
         + [
             pltpu.VMEM((1024, 128), jnp.float32),
             pltpu.VMEM((1024, 128), jnp.bfloat16),
-            pltpu.VMEM((512, 1024), jnp.bfloat16),
-            pltpu.VMEM((1024, 1024), jnp.float32),
             pltpu.VMEM((2, 128, 32, 128), jnp.bfloat16),
-            pltpu.VMEM((2, 1024, 256), jnp.bfloat16),
-            pltpu.VMEM((2, 1024, 256), jnp.bfloat16),
-            pltpu.VMEM((2, 2, 1024, 1024), jnp.float32),
-            pltpu.VMEM((2, 256, 128), jnp.float32),
             pltpu.SemaphoreType.DMA((6,)),
             pltpu.SemaphoreType.DMA,
             pltpu.SemaphoreType.DMA,
@@ -442,18 +443,60 @@
             pltpu.SemaphoreType.DMA((2,)),
         ],
         compiler_params=pltpu.CompilerParams(
-            vmem_limit_bytes=VMEM_LIMIT, collective_id=0, has_side_effects=True
+            vmem_limit_bytes=FIRST_LIMIT, collective_id=0, has_side_effects=True
         ),
         cost_estimate=pl.CostEstimate(flops=10**10, bytes_accessed=10**7, transcendentals=0),
         name="spectra",
     )(chan_map, *arrays)
 
 
+TILE = 128
+
+
+def finish_kernel(
+    lefts, rights, inverse_ref, weight_ref, before, part0, part1, part2, part3, vis_ref, power_ref, held, sems
+):
+    def copy(step):
+        rows = pl.ds(step * TILE, TILE)
+        return pltpu.make_async_copy(held.at[:, :, rows], vis_ref.at[0, :, :, rows], sems.at[step])
+
+    for step in range(1024 // TILE):
+        rows = pl.ds(step * TILE, TILE)
+        for t in range(2):
+            for part, lhs in enumerate((lefts, rights)):
+                value = lax.dot_general(lhs[t, rows, :], lefts[t], NT, preferred_element_type=jnp.float32)
+                value = (value + (part0, part1, part2, part3)[2 * t + part][rows, :]) * inverse_ref[rows, :]
+                held[t, part, rows, :] = value.astype(jnp.bfloat16)
+        copy(step).start()
+    beam_share(weight_ref, lefts, power_ref, before)
+    for step in range(1024 // TILE):
+        copy(step).wait()
+
+
+def finish(*arrays):
+    whole = pl.BlockSpec(memory_space=pltpu.VMEM)
+    return pl.pallas_call(
+        finish_kernel,
+        out_shape=(
+            jax.ShapeDtypeStruct((1, 2, 2, 1024, 1024), jnp.bfloat16),
+            jax.ShapeDtypeStruct((2, 32, 256), jnp.float32),
+        ),
+        in_specs=[whole] * len(arrays),
+        out_specs=(pl.BlockSpec(memory_space=pl.ANY), whole),
+        scratch_shapes=[
+            pltpu.VMEM((2, 2, 1024, 1024), jnp.bfloat16),
+            pltpu.SemaphoreType.DMA((1024 // TILE,)),
+        ],
+        compiler_params=pltpu.CompilerParams(vmem_limit_bytes=LAST_LIMIT),
+        cost_estimate=pl.CostEstimate(flops=3 * 10**9, bytes_accessed=10**7, transcendentals=0),
+        name="finish",
+    )(*arrays)
+
+
 def per_device(voltages, history, pfb_taps, chan_map, flag_lists, beam_index, beam_table):
     twist, dft = tables()
-    visibilities, power = spectra(
-        chan_map, voltages, history, pfb_taps, twist, dft, flag_lists.T, beam_index, beam_table
-    )
+    shares = spectra(chan_map, voltages, history, pfb_taps, twist, dft, flag_lists.T, beam_index, beam_table)
+    visibilities, power = finish(*shares)
     return visibilities, power.transpose(0, 2, 1)
 
 

time: 68.6 us -> 66.6 us (0.971)
  local copies, waits for them, and re-layouts: 4.03 us -> 0 us
  Pallas kernels: 63.8 us -> 65.7 us
    unnamed x2 -> x0, local copies, waits for them, and re-layouts: 4.03 us -> none
    pallas_call x1 -> x2, Pallas kernels: 63.8 us -> 65.7 us  [the longest x1 57.7 us: spectra(): pl.pallas_call(spectra_kernel, out_shape=(pltpu.VMEM((2, 1024, 256), jnp....]
where the time goes in v4:
time: 66.6 us; the launch traced here: 66.5 us
  Pallas kernels  65.7 us (99%)
  between operations  0.8 us (1%)
    pallas_call x1, Pallas kernels, spectra(): pl.pallas_call(spectra_kernel, out_shape=(pltpu.VMEM((2, 1024, 256), jnp....  57.7 us
    pallas_call x1, Pallas kernels, finish(): pl.pallas_call(finish_kernel, out_shape=(jax.ShapeDtypeStruct((1, 2, 2, 1...  7.99 us

profile of v4, /device:TPU:1, one launch (start us, length us, event | category | flops | bytes accessed | tf_op | source)
XLA Modules:
  0.0 66.5 jit_solution(2862317821979401772)
XLA Ops:
  0.6 57.7 %spectra.1 = (bf16[2,1024,256]{2,1,0:T(8,128)(2,1)S(1)}, bf16[2,1024,256]{2,1,0:T(8,128)(2,1)S(1)}, f32[1024,1024]{1,0:T(8,128)S(1)}, bf16[512,1024]{1,0:T(8,128...) custom-call(s32[4096]{0:T(1024)} %chan_ref.1, ...), custom_call_target="tpu_custom_call" | custom-call | flops 10000000000 | bytes 10000000 | tf_op jit(solution)/shard_map/spectra/pallas_call | solution.py:411
  58.3 8.0 %finish.1 = (bf16[1,2,2,1024,1024]{4,3,2,1,0:T(8,128)(2,1)}, f32[2,32,256]{2,1,0:T(8,128)}) custom-call(bf16[2,1024,256]{2,1,0:T(8,128)(2,1)S(1)} %get-tuple-element.13.lefts, bf16[2,1024,256]{2,1,0:T(8,128)(2,1)S(1)} %get-tuple-element.14.rights, f32[1024,1024]{1,0:T(8,128)S(1)} %get-tuple-element.15.inverse_ref, ...), custom_call_target="tpu_custom_call" | custom-call | flops 3000000000 | bytes 10000000 | tf_op jit(solution)/shard_map/finish/pallas_call | solution.py:478

commit v5 on v4

--- a/solution.py
+++ b/solution.py
@@ -342,10 +342,8 @@
     def _(step):
         rows = pl.ds(pl.multiple_of(step * 256, 256), 256)
         for t in range(2):
-            for part, lhs in enumerate((lefts, rights)):
-                (part0, part1, part2, part3)[2 * t + part][rows, :] = lax.dot_general(
-                    lhs[t, rows, :], lefts[t], NT, preferred_element_type=jnp.float32
-                )
+            for part, value in enumerate(products(t, rows, lefts, rights)):
+                (part0, part1, part2, part3)[2 * t + part][rows, :] = value
 
     beam_share(weight_ref, lefts, beam_sum)
     after.wait_send()
@@ -384,6 +382,12 @@
             lanes = pl.ds(g % 2 * 128, 128)
             lefts[g // 2, rows, lanes] = masked.astype(jnp.bfloat16)
             rights[g // 2, rows, lanes] = jnp.where(lane < 64, crossed, -crossed).astype(jnp.bfloat16)
+
+
+def products(t, rows, lefts, rights):
+    both = jnp.concatenate([lefts[t, rows, :], rights[t, rows, :]], axis=0)
+    value = lax.dot_general(both, lefts[t], NT, preferred_element_type=jnp.float32)
+    return value[: rows.size], value[rows.size :]
 
 
 def beam_share(weight_ref, lefts, beam_sum, before=None):
@@ -463,8 +467,8 @@
     for step in range(1024 // TILE):
         rows = pl.ds(step * TILE, TILE)
         for t in range(2):
-            for part, lhs in enumerate((lefts, rights)):
-                value = lax.dot_general(lhs[t, rows, :], lefts[t], NT, preferred_element_type=jnp.float32)
+            values = products(t, rows, lefts, rights)
+            for part, value in enumerate(values):
                 value = (value + (part0, part1, part2, part3)[2 * t + part][rows, :]) * inverse_ref[rows, :]
                 held[t, part, rows, :] = value.astype(jnp.bfloat16)
         copy(step).start()

time: 66.6 us -> 63 us (0.946)
  Pallas kernels: 65.7 us -> 62.2 us
    pallas_call x1, Pallas kernels: 7.99 us -> 4.75 us  [finish(): pl.pallas_call(finish_kernel, out_shape=(jax.ShapeDtypeStruct((1, 2, 2, 1...]
where the time goes in v5:
time: 63 us; the launch traced here: 62.9 us
  Pallas kernels  62.2 us (99%)
  between operations  0.64 us (1%)
    pallas_call x1, Pallas kernels, spectra(): pl.pallas_call(spectra_kernel, out_shape=(pltpu.VMEM((2, 1024, 256), jnp....  57.5 us
    pallas_call x1, Pallas kernels, finish(): pl.pallas_call(finish_kernel, out_shape=(jax.ShapeDtypeStruct((1, 2, 2, 1...  4.75 us

profile of v5, /device:TPU:1, one launch (start us, length us, event | category | flops | bytes accessed | tf_op | source)
XLA Modules:
  0.0 62.9 jit_solution(10167151994641720181)
XLA Ops:
  0.6 57.5 %spectra.1 = (bf16[2,1024,256]{2,1,0:T(8,128)(2,1)S(1)}, bf16[2,1024,256]{2,1,0:T(8,128)(2,1)S(1)}, f32[1024,1024]{1,0:T(8,128)S(1)}, bf16[512,1024]{1,0:T(8,128...) custom-call(s32[4096]{0:T(1024)} %chan_ref.1, ...), custom_call_target="tpu_custom_call" | custom-call | flops 10000000000 | bytes 10000000 | tf_op jit(solution)/shard_map/spectra/pallas_call | solution.py:415
  58.1 4.7 %finish.1 = (bf16[1,2,2,1024,1024]{4,3,2,1,0:T(8,128)(2,1)}, f32[2,32,256]{2,1,0:T(8,128)}) custom-call(bf16[2,1024,256]{2,1,0:T(8,128)(2,1)S(1)} %get-tuple-element.13.lefts, bf16[2,1024,256]{2,1,0:T(8,128)(2,1)S(1)} %get-tuple-element.14.rights, f32[1024,1024]{1,0:T(8,128)S(1)} %get-tuple-element.15.inverse_ref, ...), custom_call_target="tpu_custom_call" | custom-call | flops 3000000000 | bytes 10000000 | tf_op jit(solution)/shard_map/finish/pallas_call | solution.py:482

commit v6 on v5

--- a/solution.py
+++ b/solution.py
@@ -1,3 +1,4 @@
+import functools
 import math
 
 import numpy as np
@@ -177,7 +178,7 @@
     lefts, rights, inverse_ref, weight_ref, beam_sum, part0, part1, part2, part3,
     src, mid, high, low, lines, picked, out, taps_ref, twist_ref, dft_ref, flags_ref, index_ref, table_ref,
     twice, mask_ref, arrived,
-    load_sem, own_sem, rim_sem, halo_send, halo_recv, send_sem, recv_sem,
+    load_sem, own_sem, rim_sem, halo_send, halo_recv, send_sem, recv_sem, entered,
 ):
     grp, dev = lax.axis_index("grp"), lax.axis_index("dev")
     n_grp, n_dev = lax.axis_size("grp"), lax.axis_size("dev")
@@ -188,19 +189,14 @@
     is_first, is_last = grp == 0, grp == n_grp - 1
     barrier = pltpu.get_barrier_semaphore()
 
-    for n in (1, 3, 2, 0):
-
-        @pl.loop(0, n_dev, unroll=8)
-        def _(peer):
-            def greet():
-                pl.semaphore_signal(
-                    barrier, inc=1, device_id=(planes[n], peer), device_id_type=pl.DeviceIdType.MESH
-                )
-
-            if n:
-                greet()
-            else:
-                pl.when(peer != dev)(greet)
+    for n in range(1, n_grp):
+        pl.semaphore_signal(barrier, inc=1, device_id=(planes[n], dev), device_id_type=pl.DeviceIdType.MESH)
+
+    @pl.loop(0, n_dev, unroll=8)
+    def _(peer):
+        @pl.when(peer != dev)
+        def _():
+            pl.semaphore_signal(barrier, inc=1, device_id=(grp, peer), device_id_type=pl.DeviceIdType.MESH)
 
     def blocks(ref, start, number, rows=slice(None)):
         return ref.at[:, rows, pl.ds(pl.multiple_of(start * BLK, BLK), number * BLK)]
@@ -244,7 +240,7 @@
     near = halo(3, 1, pl.ds(0, 32), 1, right)
     far = halo(2, 0, low_rows, 2, right)
 
-    pl.semaphore_wait(barrier, count - 1)
+    pl.semaphore_wait(barrier, n_grp + n_dev - 2)
     after.start()
 
     @pl.when(jnp.logical_not(is_last))
@@ -256,6 +252,9 @@
     @pl.when(jnp.logical_not(is_last))
     def _():
         far.start()
+
+    for n in range(1, n_grp):
+        pl.semaphore_signal(entered, inc=1, device_id=(planes[n], dev), device_id_type=pl.DeviceIdType.MESH)
 
     for load in loads:
         load.wait()
@@ -314,6 +313,7 @@
 
     after.wait_recv()
     both_halves(jnp.where(is_last, 8, 3), 32)
+    pl.semaphore_wait(entered, n_grp - 1)
     send_batch(0)
 
     @pl.when(is_first)
@@ -445,6 +445,7 @@
             pltpu.SemaphoreType.DMA((4,)),
             pltpu.SemaphoreType.DMA((2,)),
             pltpu.SemaphoreType.DMA((2,)),
+            pltpu.SemaphoreType.REGULAR,
         ],
         compiler_params=pltpu.CompilerParams(
             vmem_limit_bytes=FIRST_LIMIT, collective_id=0, has_side_effects=True

time: 63 us -> 61.8 us (0.981)
  Pallas kernels: 62.2 us -> 61 us
    pallas_call x1, Pallas kernels: 57.5 us -> 56.3 us  [spectra(): pl.pallas_call(spectra_kernel, out_shape=(pltpu.VMEM((2, 1024, 256), jnp....]
where the time goes in v6:
time: 61.8 us; the launch traced here: 61.7 us
  Pallas kernels  61 us (99%)
  between operations  0.64 us (1%)
    pallas_call x1, Pallas kernels, spectra(): pl.pallas_call(spectra_kernel, out_shape=(pltpu.VMEM((2, 1024, 256), jnp....  56.3 us
    pallas_call x1, Pallas kernels, finish(): pl.pallas_call(finish_kernel, out_shape=(jax.ShapeDtypeStruct((1, 2, 2, 1...  4.75 us

profile of v6, /device:TPU:1, one launch (start us, length us, event | category | flops | bytes accessed | tf_op | source)
XLA Modules:
  0.0 61.7 jit_solution(3470699681707932269)
XLA Ops:
  0.6 56.3 %spectra.1 = (bf16[2,1024,256]{2,1,0:T(8,128)(2,1)S(1)}, bf16[2,1024,256]{2,1,0:T(8,128)(2,1)S(1)}, f32[1024,1024]{1,0:T(8,128)S(1)}, bf16[512,1024]{1,0:T(8,128...) custom-call(s32[4096]{0:T(1024)} %chan_ref.1, ...), custom_call_target="tpu_custom_call" | custom-call | flops 10000000000 | bytes 10000000 | tf_op jit(solution)/shard_map/spectra/pallas_call | solution.py:415
  56.9 4.7 %finish.1 = (bf16[1,2,2,1024,1024]{4,3,2,1,0:T(8,128)(2,1)}, f32[2,32,256]{2,1,0:T(8,128)}) custom-call(bf16[2,1024,256]{2,1,0:T(8,128)(2,1)S(1)} %get-tuple-element.13.lefts, bf16[2,1024,256]{2,1,0:T(8,128)(2,1)S(1)} %get-tuple-element.14.rights, f32[1024,1024]{1,0:T(8,128)S(1)} %get-tuple-element.15.inverse_ref, ...), custom_call_target="tpu_custom_call" | custom-call | flops 3000000000 | bytes 10000000 | tf_op jit(solution)/shard_map/finish/pallas_call | solution.py:483

commit v7 on v6

--- a/solution.py
+++ b/solution.py
@@ -1,4 +1,3 @@
-import functools
 import math
 
 import numpy as np
@@ -247,12 +246,6 @@
     def _():
         near.start()
 
-    beyond.start()
-
-    @pl.when(jnp.logical_not(is_last))
-    def _():
-        far.start()
-
     for n in range(1, n_grp):
         pl.semaphore_signal(entered, inc=1, device_id=(planes[n], dev), device_id_type=pl.DeviceIdType.MESH)
 
@@ -268,10 +261,10 @@
             filtered(window, line, pl.multiple_of(half * 16, 16))
 
     def send_batch(batch):
-        @pl.loop(0, N1 // 8)
+        @pl.loop(0, N1 // 16)
         def _(step):
-            for n in range(8):
-                second_stage(step * 8 + n, dft_ref, high, low, lines)
+            for n in range(16):
+                second_stage(step * 16 + n, dft_ref, high, low, lines)
 
         @pl.loop(0, 8)
         def _(step):
@@ -307,6 +300,14 @@
     both_halves(2, 0)
     side_work(me, chan_ref, flags_ref, index_ref, table_ref, mask_ref, weight_ref, inverse_ref, twice)
 
+    after.wait_send()
+    beyond.start()
+
+    @pl.when(jnp.logical_not(is_last))
+    def _():
+        near.wait_send()
+        far.start()
+
     @pl.when(is_last)
     def _():
         rim_last.wait()
@@ -346,12 +347,10 @@
                 (part0, part1, part2, part3)[2 * t + part][rows, :] = value
 
     beam_share(weight_ref, lefts, beam_sum)
-    after.wait_send()
     beyond.wait_send()
 
     @pl.when(jnp.logical_not(is_last))
     def _():
-        near.wait_send()
         far.wait_send()
 
     for batch in range(2):

time: 61.8 us -> 61.2 us (level)
  Pallas kernels: 61 us -> 60.3 us
    pallas_call x1, Pallas kernels: 56.3 us -> 55.6 us  [spectra(): pl.pallas_call(spectra_kernel, out_shape=(pltpu.VMEM((2, 1024, 256), jnp....]
where the time goes in v7:
time: 61.2 us; the launch traced here: 61 us
  Pallas kernels  60.3 us (99%)
  between operations  0.64 us (1%)
    pallas_call x1, Pallas kernels, spectra(): pl.pallas_call(spectra_kernel, out_shape=(pltpu.VMEM((2, 1024, 256), jnp....  55.6 us
    pallas_call x1, Pallas kernels, finish(): pl.pallas_call(finish_kernel, out_shape=(jax.ShapeDtypeStruct((1, 2, 2, 1...  4.75 us

profile of v7, /device:TPU:1, one launch (start us, length us, event | category | flops | bytes accessed | tf_op | source)
XLA Modules:
  0.0 61.0 jit_solution(6653529570856970410)
XLA Ops:
  0.6 55.6 %spectra.1 = (bf16[2,1024,256]{2,1,0:T(8,128)(2,1)S(1)}, bf16[2,1024,256]{2,1,0:T(8,128)(2,1)S(1)}, f32[1024,1024]{1,0:T(8,128)S(1)}, bf16[512,1024]{1,0:T(8,128...) custom-call(s32[4096]{0:T(1024)} %chan_ref.1, ...), custom_call_target="tpu_custom_call" | custom-call | flops 10000000000 | bytes 10000000 | tf_op jit(solution)/shard_map/spectra/pallas_call | solution.py:414
  56.2 4.7 %finish.1 = (bf16[1,2,2,1024,1024]{4,3,2,1,0:T(8,128)(2,1)}, f32[2,32,256]{2,1,0:T(8,128)}) custom-call(bf16[2,1024,256]{2,1,0:T(8,128)(2,1)S(1)} %get-tuple-element.13.lefts, bf16[2,1024,256]{2,1,0:T(8,128)(2,1)S(1)} %get-tuple-element.14.rights, f32[1024,1024]{1,0:T(8,128)S(1)} %get-tuple-element.15.inverse_ref, ...), custom_call_target="tpu_custom_call" | custom-call | flops 3000000000 | bytes 10000000 | tf_op jit(solution)/shard_map/finish/pallas_call | solution.py:482
